TPU v7x, 512 devices: a whole 4x8x8 slice. The times are simulated.
512 devices in a mesh: gz: 128 (over z, y, core), col: 4 (over x).
Axes of the slice: x: 4, y: 8, z: 8, core: 2. Of those that a mesh axis runs over, the one named last changes fastest.
Arguments:
- populations: bfloat16 [19, 256, 32, 512], P(None, 'gz', 'col'), may hold values from 0.5 to 1.5
- solid: int32 [256, 32, 512], P('gz', 'col'), may hold values 0 or 1
- radius: float32 [131072], P(('gz', 'col')), may hold values from 0.5 to 1.5
- rate: float32 [131072], P(('gz', 'col')), may hold values from 0.1 to 1
- ice_mass: float32 [131072], P(('gz', 'col')), may hold values from 1 to 3
- owner: int32 [131072, 1], P(('gz', 'col')), may hold values from 0 to 127; in each aligned block of 256 rows (0 to 255, 256 to 511, ...) at most 4 rows name the same one
- voxel: int32 [131072], P(('gz', 'col')), may hold values from 0 to 8191
Outputs:
- new_populations: bfloat16 [19, 256, 32, 512], P(None, 'gz', 'col')
- flux: float32 [131072], P(('gz', 'col'))
- ice_left: float32 [131072], P(('gz', 'col'))
Inputs may be any that keep to these rules, and one draw needn't show every extreme that they name: Among the 256 records of one device at most 4 name the same owner, and some device reaches 4.
All inputs are finite; a program needn't handle non-finite values. No bound on the sum of `solid` on one device may be relied on, other than what follows from the above.
Results may differ from a plain program's by a relative error of at most 0.0041.
Values may be sent and summed in bfloat16 or wider, within the bound.
A program may use at most 64 MiB of HBM per device.

v0:
```python
import jax
import jax.numpy as jnp
from jax import lax
from jax.sharding import PartitionSpec as P

STEPS = 2


VELOCITIES = [
    (0, 0, 0),
    (1, 0, 0),
    (-1, 0, 0),
    (0, 1, 0),
    (0, -1, 0),
    (0, 0, 1),
    (0, 0, -1),
    (1, 1, 0),
    (-1, -1, 0),
    (1, -1, 0),
    (-1, 1, 0),
    (1, 0, 1),
    (-1, 0, -1),
    (1, 0, -1),
    (-1, 0, 1),
    (0, 1, 1),
    (0, -1, -1),
    (0, 1, -1),
    (0, -1, 1),
]
OPPOSITE = [0, 2, 1, 4, 3, 6, 5, 8, 7, 10, 9, 12, 11, 14, 13, 16, 15, 18, 17]
LATTICE_WEIGHTS = [1.0 / 3.0] + [1.0 / 18.0] * 6 + [1.0 / 36.0] * 12
OMEGA = 1.6


def extended(array, sides, width):
    for axis, dim in sides:
        size, length = (lax.axis_size(axis), array.shape[dim])
        up = [(i, (i + 1) % size) for i in range(size - 1)]
        down = [(j, i) for i, j in up]
        last = lax.slice_in_dim(array, length - width, length, axis=dim)
        leading = lax.slice_in_dim(array, 0, width, axis=dim)
        before = lax.ppermute(last, axis, up)
        after = lax.ppermute(leading, axis, down)
        array = jnp.concatenate([before, array, after], axis=dim)
    return array


def moment_table():
    rows = [LATTICE_WEIGHTS]
    for axis_pos in range(3):
        rows.append([LATTICE_WEIGHTS[q] * VELOCITIES[q][axis_pos] for q in range(19)])
    return jnp.array(rows, jnp.float32)


def moments(values):
    return jnp.tensordot(moment_table(), values, axes=1, precision=lax.Precision.HIGHEST)


def collide(pops, solid_flag, source):
    values = pops.astype(jnp.float32)
    stats = moments(values)
    density = stats[0]
    velocity = stats[1:] / density
    along = jnp.tensordot(
        jnp.array(VELOCITIES, jnp.float32), velocity, axes=1, precision=lax.Precision.HIGHEST
    )
    square = jnp.sum(velocity * velocity, 0)
    balance = density * (1.0 + 3.0 * along + 4.5 * along * along - 1.5 * square)
    relaxed = values - OMEGA * (values - balance) + source.astype(jnp.float32)
    bounced = jnp.stack([values[k] for k in OPPOSITE])
    result = jnp.where(solid_flag, bounced, relaxed)
    return result.astype(jnp.bfloat16)


def stream(padded):
    depth = padded.shape[1] - 2
    across = padded.shape[2] - 2
    moved = []
    for q in range(19):
        cz, cx, cy = VELOCITIES[q]
        piece = padded[q, 1 - cz : 1 - cz + depth, 1 - cx : 1 - cx + across, :]
        moved.append(jnp.roll(piece, cy, axis=2))
    return jnp.stack(moved)


def body(populations, solid, radius, rate, ice_mass, owner, voxel):
    planes, across, width = solid.shape
    density0 = moments(populations.astype(jnp.float32))[0].reshape(-1)
    coef = rate * radius * radius
    owners = lax.axis_size("gz")
    count = coef.shape[0]
    accum = jnp.zeros((planes * across * width,), jnp.float32)
    capacity = max(2, 2 * count // owners)
    target = owner[:, 0]
    onehot = (target[:, None] == jnp.arange(owners, dtype=jnp.int32)[None, :]).astype(jnp.int32)
    before = jnp.cumsum(onehot, 0) - onehot
    slot_rank = jnp.sum(before * onehot, 1)
    position = target * capacity + slot_rank
    sent_coef = jnp.zeros((owners * capacity,), jnp.float32).at[position].set(coef)
    sent_cell = (
        jnp.zeros((owners * capacity,), jnp.float32).at[position].set(voxel.astype(jnp.float32))
    )
    got_coef, got_cell = (
        lax.all_to_all(sent_coef, "gz", split_axis=0, concat_axis=0, tiled=True),
        lax.all_to_all(sent_cell, "gz", split_axis=0, concat_axis=0, tiled=True),
    )
    cells = got_cell.astype(jnp.int32)
    answer = got_coef * (2.0 - density0[cells])
    accum = accum.at[cells].add(0.5 * answer)
    back = lax.all_to_all(answer, "gz", split_axis=0, concat_axis=0, tiled=True)
    flux = back[position]
    source = accum.reshape(planes, across, width).astype(jnp.bfloat16)
    solid_flag = solid > 0
    state = populations
    for step in range(STEPS):
        post = collide(state, solid_flag, source)
        padded = extended(post, (("gz", 1), ("col", 2)), 1)
        state = stream(padded)
    return (state, flux, ice_mass - flux)


def solution(mesh):
    return jax.shard_map(
        body,
        mesh=mesh,
        in_specs=(
            P(None, "gz", "col", None),
            P("gz", "col", None),
            P(("gz", "col")),
            P(("gz", "col")),
            P(("gz", "col")),
            P(("gz", "col"), None),
            P(("gz", "col")),
        ),
        out_specs=(P(None, "gz", "col", None), P(("gz", "col")), P(("gz", "col"))),
        check_vma=False,
    )
```

profile of v0, /device:TPU:1, one launch (start us, length us, event | category | flops | bytes accessed | tf_op | source)
XLA Modules:
  0.0 130.0 jit_solution(14263291511193744674)
XLA Ops:
  2.6 1.4 %scatter_custom_fusion = f32[512]{0:T(512)S(1)} fusion(s32[256]{0:T(256)S(1)} %bitcast.178, f32[256]{0:T(256)S(1)} %convert_element_type.58, f32[]{:T(128)} %constant.18.clone.1), kind=kCustom, calls=%fused_computation.146 | custom fusion | bytes 2052 | tf_op jit(solution)/shard_map/scatter | solution.py:101
  4.7 18.4 %all-to-all-start = ((f32[128,4,1]{1,2,0:T(1,128)}), f32[128,4,1]{1,2,0:T(1,128)S(1)}, u32[]{:S(2)}, u32[]{:S(2)}) async-start(f32[128,4,1]{1,2,0:T(1,128)} %bitcast.11), calls=%async_computation | async-start | bytes 131072 | tf_op jit(solution)/shard_map/all_to_all | solution.py:105
  26.2 1.4 %scatter_custom_fusion.1 = f32[512]{0:T(512)S(1)} fusion(s32[256]{0:T(256)S(1)} %bitcast.179, f32[256]{0:T(256)S(1)} %multiply_multiply_fusion.3, f32[]{:T(128)} %constant.18.clone.1), kind=kCustom, calls=%fused_computation.144 | custom fusion | bytes 2052 | tf_op jit(solution)/shard_map/scatter | solution.py:99
  28.3 0.9 stack.90
  29.2 5.4 %all-to-all-done = f32[128,4,1]{1,2,0:T(1,128)S(1)} async-done(((f32[128,4,1]{1,2,0:T(1,128)}), f32[128,4,1]{1,2,0:T(1,128)S(1)}, u32[]{:S(2)}, u32[]{:S(2)}) %all-to-all-start) | async-done | bytes 2080 | tf_op jit(solution)/shard_map/all_to_all | solution.py:105
  34.6 8.4 %all-to-all-start.1 = ((f32[128,4,1]{1,2,0:T(1,128)}), f32[128,4,1]{1,2,0:T(1,128)S(1)}, u32[]{:S(2)}, u32[]{:S(2)}) async-start(f32[128,4,1]{1,2,0:T(1,128)} %bitcast.13), calls=%async_computation.1 | async-start | bytes 131072 | tf_op jit(solution)/shard_map/all_to_all | solution.py:104
  43.3 11.1 %all-to-all-done.1 = f32[128,4,1]{1,2,0:T(1,128)S(1)} async-done(((f32[128,4,1]{1,2,0:T(1,128)}), f32[128,4,1]{1,2,0:T(1,128)S(1)}, u32[]{:S(2)}, u32[]{:S(2)}) %all-to-all-start.1) | async-done | bytes 2080 | tf_op jit(solution)/shard_map/all_to_all | solution.py:104
  54.9 0.8 reduce.10
  55.8 3.1 %gather_fusion = f32[512]{0:T(512)S(1)} fusion(f32[8192]{0:T(1024)S(1)} %bitcast.140, s32[1024]{0:T(1024)S(1)} %pad_clamp_fusion.1), kind=kCustom, calls=%fused_computation | custom fusion | bytes 6144 | tf_op jit(solution)/shard_map/gather | solution.py:108
  59.0 3.3 %scatter_custom_fusion.2 = f32[8192]{0:T(1024)S(1)} fusion(s32[512]{0:T(512)S(1)} %bitcast.176, f32[512]{0:T(512)S(1)} %get-tuple-element.110, f32[]{:T(128)} %constant.18.clone.1), kind=kCustom, calls=%fused_computation.131 | custom fusion | flops 512 | bytes 32772 | tf_op jit(solution)/shard_map/scatter-add | solution.py:109
  63.0 1.3 fusion.8
  64.3 2.7 %collective-permute-start.1 = (bf16[19,1,8,512]{3,0,2,1:T(8,128)(2,1)S(1)}, bf16[19,1,8,512]{3,0,2,1:T(8,128)(2,1)S(1)}, u32[]{:S(2)}, u32[]{:S(2)}) collective-permute-start(bf16[19,1,8,512]{3,0,2,1:T(8,128)(2,1)S(1)} %get-tuple-element.88), channel_id=1, source_target_pairs={{4,0},{8,4},{12,8},{16,12},{20,16},{24,20},{28,24},{32,28},{36,32}... | collective-permute-start | bytes 466952 | tf_op jit(solution)/shard_map/ppermute | solution.py:43
  67.0 3.1 %collective-permute-start = (bf16[19,1,8,512]{3,0,2,1:T(8,128)(2,1)S(1)}, bf16[19,1,8,512]{3,0,2,1:T(8,128)(2,1)S(1)}, u32[]{:S(2)}, u32[]{:S(2)}) collective-permute-start(bf16[19,1,8,512]{3,0,2,1:T(8,128)(2,1)S(1)} %get-tuple-element.89), channel_id=1, source_target_pairs={{0,4},{4,8},{8,12},{12,16},{16,20},{20,24},{24,28},{28,32},{32,36}... | collective-permute-start | bytes 466952 | tf_op jit(solution)/shard_map/ppermute | solution.py:42
  70.1 1.4 %collective-permute-done.1 = bf16[19,1,8,512]{3,0,2,1:T(8,128)(2,1)S(1)} collective-permute-done((bf16[19,1,8,512]{3,0,2,1:T(8,128)(2,1)S(1)}, bf16[19,1,8,512]{3,0,2,1:T(8,128)(2,1)S(1)}, u32[]{:S(2)}, u32[]{:S(2)}) %collective-permute-start.1) | collective-permute-done | bytes 155680 | tf_op jit(solution)/shard_map/ppermute | solution.py:43
  71.5 1.2 collective-permute-done
  72.7 1.3 collective-permute-start.3
  74.0 4.0 %collective-permute-start.2 = (bf16[19,4,1,512]{3,0,2,1:T(8,128)(2,1)S(1)}, bf16[19,4,1,512]{3,0,2,1:T(8,128)(2,1)S(1)}, u32[]{:S(2)}, u32[]{:S(2)}) collective-permute-start(bf16[19,4,1,512]{3,0,2,1:T(8,128)(2,1)S(1)} %get-tuple-element.44), channel_id=1, source_target_pairs={{0,1},{1,2},{2,3},{4,5},{5,6},{6,7},{8,9},{9,10},{10,11},{12,13},{... | collective-permute-start | bytes 233480 | tf_op jit(solution)/shard_map/ppermute | solution.py:42
  78.3 1.3 collective-permute-done.2
  82.0 0.9 stack.101
  84.0 0.9 stack.102
  84.9 1.2 fusion.17
  86.2 1.9 %collective-permute-start.5 = (bf16[19,1,8,512]{3,0,2,1:T(8,128)(2,1)S(1)}, bf16[19,1,8,512]{3,0,2,1:T(8,128)(2,1)S(1)}, u32[]{:S(2)}, u32[]{:S(2)}) collective-permute-start(bf16[19,1,8,512]{3,0,2,1:T(8,128)(2,1)S(1)} %get-tuple-element.64), channel_id=1, source_target_pairs={{4,0},{8,4},{12,8},{16,12},{20,16},{24,20},{28,24},{32,28},{36,32}... | collective-permute-start | bytes 466952 | tf_op jit(solution)/shard_map/ppermute | solution.py:43
  88.1 5.5 %collective-permute-start.4 = (bf16[19,1,8,512]{3,0,2,1:T(8,128)(2,1)S(1)}, bf16[19,1,8,512]{3,0,2,1:T(8,128)(2,1)S(1)}, u32[]{:S(2)}, u32[]{:S(2)}) collective-permute-start(bf16[19,1,8,512]{3,0,2,1:T(8,128)(2,1)S(1)} %get-tuple-element.65), channel_id=1, source_target_pairs={{0,4},{4,8},{8,12},{12,16},{16,20},{20,24},{24,28},{28,32},{32,36}... | collective-permute-start | bytes 466952 | tf_op jit(solution)/shard_map/ppermute | solution.py:42
  94.7 10.7 %all-to-all-start.2 = ((f32[128,4,1]{1,2,0:T(1,128)}), f32[128,4,1]{1,2,0:T(1,128)S(1)}, u32[]{:S(2)}, u32[]{:S(2)}) async-start(f32[128,4,1]{1,2,0:T(1,128)} %copy.395), calls=%async_computation.2 | async-start | bytes 131072 | tf_op jit(solution)/shard_map/all_to_all | solution.py:110
  105.4 1.3 collective-permute-start.7
  106.7 10.0 %all-to-all-done.2 = f32[128,4,1]{1,2,0:T(1,128)S(1)} async-done(((f32[128,4,1]{1,2,0:T(1,128)}), f32[128,4,1]{1,2,0:T(1,128)S(1)}, u32[]{:S(2)}, u32[]{:S(2)}) %all-to-all-start.2) | async-done | bytes 2080 | tf_op jit(solution)/shard_map/all_to_all | solution.py:110
  116.7 0.8 reduce.11
  117.6 1.9 %gather_fusion.1 = f32[256]{0:T(256)S(1)} fusion(f32[512]{0:T(512)S(1)} %all_to_all.26, s32[1024]{0:T(1024)S(1)} %pad_clamp_fusion), kind=kCustom, calls=%fused_computation.1 | custom fusion | bytes 3072 | tf_op jit(solution)/shard_map/gather | solution.py:111
  120.2 4.0 %collective-permute-start.6 = (bf16[19,4,1,512]{3,0,2,1:T(8,128)(2,1)S(1)}, bf16[19,4,1,512]{3,0,2,1:T(8,128)(2,1)S(1)}, u32[]{:S(2)}, u32[]{:S(2)}) collective-permute-start(bf16[19,4,1,512]{3,0,2,1:T(8,128)(2,1)S(1)} %get-tuple-element.40), channel_id=1, source_target_pairs={{0,1},{1,2},{2,3},{4,5},{5,6},{6,7},{8,9},{9,10},{10,11},{12,13},{... | collective-permute-start | bytes 233480 | tf_op jit(solution)/shard_map/ppermute | solution.py:42
  124.5 1.3 %collective-permute-done.6 = bf16[19,4,1,512]{3,0,2,1:T(8,128)(2,1)S(1)} collective-permute-done((bf16[19,4,1,512]{3,0,2,1:T(8,128)(2,1)S(1)}, bf16[19,4,1,512]{3,0,2,1:T(8,128)(2,1)S(1)}, u32[]{:S(2)}, u32[]{:S(2)}) %collective-permute-start.6) | collective-permute-done | bytes 77856 | tf_op jit(solution)/shard_map/ppermute | solution.py:42
  128.2 0.9 stack.113
  129.1 0.8 copy.396
  (164 shorter events, 15.9 us)
Async XLA Ops:
  0.6 0.7 copy-start.2
  1.7 21.5 %copy-start = (bf16[19,2,8,512]{3,2,1,0:T(8,128)(2,1)S(1)}, bf16[19,2,8,512]{3,2,1,0:T(8,128)(2,1)}, u32[]{:S(2)}) copy-start(bf16[19,2,8,512]{3,2,1,0:T(8,128)(2,1)} %param.12) | copy-start | bytes 933892
  1.9 0.7 copy-start.8
  4.7 29.8 %all-to-all-start = ((f32[128,4,1]{1,2,0:T(1,128)}), f32[128,4,1]{1,2,0:T(1,128)S(1)}, u32[]{:S(2)}, u32[]{:S(2)}) async-start(f32[128,4,1]{1,2,0:T(1,128)} %bitcast.11), calls=%async_computation | async-start | bytes 131072 | tf_op jit(solution)/shard_map/all_to_all | solution.py:105
  23.4 0.7 copy-start.3
  24.7 0.8 copy-start.1
  25.5 0.7 copy-start.5
  25.5 0.7 copy-start.6
  34.6 19.8 %all-to-all-start.1 = ((f32[128,4,1]{1,2,0:T(1,128)}), f32[128,4,1]{1,2,0:T(1,128)S(1)}, u32[]{:S(2)}, u32[]{:S(2)}) async-start(f32[128,4,1]{1,2,0:T(1,128)} %bitcast.13), calls=%async_computation.1 | async-start | bytes 131072 | tf_op jit(solution)/shard_map/all_to_all | solution.py:104
  62.3 0.7 copy-start.9
  64.3 7.2 %collective-permute-start.1 = (bf16[19,1,8,512]{3,0,2,1:T(8,128)(2,1)S(1)}, bf16[19,1,8,512]{3,0,2,1:T(8,128)(2,1)S(1)}, u32[]{:S(2)}, u32[]{:S(2)}) collective-permute-start(bf16[19,1,8,512]{3,0,2,1:T(8,128)(2,1)S(1)} %get-tuple-element.88), channel_id=1, source_target_pairs={{4,0},{8,4},{12,8},{16,12},{20,16},{24,20},{28,24},{32,28},{36,32}... | collective-permute-start | bytes 466952 | tf_op jit(solution)/shard_map/ppermute | solution.py:43
  67.0 5.7 %collective-permute-start = (bf16[19,1,8,512]{3,0,2,1:T(8,128)(2,1)S(1)}, bf16[19,1,8,512]{3,0,2,1:T(8,128)(2,1)S(1)}, u32[]{:S(2)}, u32[]{:S(2)}) collective-permute-start(bf16[19,1,8,512]{3,0,2,1:T(8,128)(2,1)S(1)} %get-tuple-element.89), channel_id=1, source_target_pairs={{0,4},{4,8},{8,12},{12,16},{16,20},{20,24},{24,28},{28,32},{32,36}... | collective-permute-start | bytes 466952 | tf_op jit(solution)/shard_map/ppermute | solution.py:42
  72.7 5.4 %collective-permute-start.3 = (bf16[19,4,1,512]{3,0,2,1:T(8,128)(2,1)S(1)}, bf16[19,4,1,512]{3,0,2,1:T(8,128)(2,1)S(1)}, u32[]{:S(2)}, u32[]{:S(2)}) collective-permute-start(bf16[19,4,1,512]{3,0,2,1:T(8,128)(2,1)S(1)} %get-tuple-element.43), channel_id=1, source_target_pairs={{1,0},{2,1},{3,2},{5,4},{6,5},{7,6},{9,8},{10,9},{11,10},{13,12},{... | collective-permute-start | bytes 233480 | tf_op jit(solution)/shard_map/ppermute | solution.py:43
  74.0 5.6 %collective-permute-start.2 = (bf16[19,4,1,512]{3,0,2,1:T(8,128)(2,1)S(1)}, bf16[19,4,1,512]{3,0,2,1:T(8,128)(2,1)S(1)}, u32[]{:S(2)}, u32[]{:S(2)}) collective-permute-start(bf16[19,4,1,512]{3,0,2,1:T(8,128)(2,1)S(1)} %get-tuple-element.44), channel_id=1, source_target_pairs={{0,1},{1,2},{2,3},{4,5},{5,6},{6,7},{8,9},{9,10},{10,11},{12,13},{... | collective-permute-start | bytes 233480 | tf_op jit(solution)/shard_map/ppermute | solution.py:42
  86.2 19.2 %collective-permute-start.5 = (bf16[19,1,8,512]{3,0,2,1:T(8,128)(2,1)S(1)}, bf16[19,1,8,512]{3,0,2,1:T(8,128)(2,1)S(1)}, u32[]{:S(2)}, u32[]{:S(2)}) collective-permute-start(bf16[19,1,8,512]{3,0,2,1:T(8,128)(2,1)S(1)} %get-tuple-element.64), channel_id=1, source_target_pairs={{4,0},{8,4},{12,8},{16,12},{20,16},{24,20},{28,24},{32,28},{36,32}... | collective-permute-start | bytes 466952 | tf_op jit(solution)/shard_map/ppermute | solution.py:43
  88.1 17.2 %collective-permute-start.4 = (bf16[19,1,8,512]{3,0,2,1:T(8,128)(2,1)S(1)}, bf16[19,1,8,512]{3,0,2,1:T(8,128)(2,1)S(1)}, u32[]{:S(2)}, u32[]{:S(2)}) collective-permute-start(bf16[19,1,8,512]{3,0,2,1:T(8,128)(2,1)S(1)} %get-tuple-element.65), channel_id=1, source_target_pairs={{0,4},{4,8},{8,12},{12,16},{16,20},{20,24},{24,28},{28,32},{32,36}... | collective-permute-start | bytes 466952 | tf_op jit(solution)/shard_map/ppermute | solution.py:42
  94.7 22.0 %all-to-all-start.2 = ((f32[128,4,1]{1,2,0:T(1,128)}), f32[128,4,1]{1,2,0:T(1,128)S(1)}, u32[]{:S(2)}, u32[]{:S(2)}) async-start(f32[128,4,1]{1,2,0:T(1,128)} %copy.395), calls=%async_computation.2 | async-start | bytes 131072 | tf_op jit(solution)/shard_map/all_to_all | solution.py:110
  105.4 18.8 %collective-permute-start.7 = (bf16[19,4,1,512]{3,0,2,1:T(8,128)(2,1)S(1)}, bf16[19,4,1,512]{3,0,2,1:T(8,128)(2,1)S(1)}, u32[]{:S(2)}, u32[]{:S(2)}) collective-permute-start(bf16[19,4,1,512]{3,0,2,1:T(8,128)(2,1)S(1)} %get-tuple-element.39), channel_id=1, source_target_pairs={{1,0},{2,1},{3,2},{5,4},{6,5},{7,6},{9,8},{10,9},{11,10},{13,12},{... | collective-permute-start | bytes 233480 | tf_op jit(solution)/shard_map/ppermute | solution.py:43
  117.6 2.0 %copy-start.7 = (f32[256]{0:T(256)S(1)}, f32[256]{0:T(256)}, u32[]{:S(2)}) copy-start(f32[256]{0:T(256)} %param.16) | copy-start | bytes 3076
  119.6 0.6 copy-start.4
  120.2 5.6 %collective-permute-start.6 = (bf16[19,4,1,512]{3,0,2,1:T(8,128)(2,1)S(1)}, bf16[19,4,1,512]{3,0,2,1:T(8,128)(2,1)S(1)}, u32[]{:S(2)}, u32[]{:S(2)}) collective-permute-start(bf16[19,4,1,512]{3,0,2,1:T(8,128)(2,1)S(1)} %get-tuple-element.40), channel_id=1, source_target_pairs={{0,1},{1,2},{2,3},{4,5},{5,6},{6,7},{8,9},{9,10},{10,11},{12,13},{... | collective-permute-start | bytes 233480 | tf_op jit(solution)/shard_map/ppermute | solution.py:42
where the time goes:
time: 132 us; the launch traced here: 130 us
  starting transfers between devices  61.2 us (46%)
  waiting for transfers between devices  31.7 us (24%)
  local copies, waits for them, and re-layouts  22.9 us (17%)
  other arithmetic  9.3 us (7%)
  matrix products  3.29 us (2%)
  between operations  1.46 us (1%)
    all_to_all x1, starting transfers between devices, body(): lax.all_to_all(sent_cell, 'gz', split_axis=0, concat_axis=0, tiled=True)  18.4 us
    ppermute x4, starting transfers between devices, extended(): before = lax.ppermute(last, axis, up)  16.6 us
    all_to_all x1, waiting for transfers between devices, body(): lax.all_to_all(sent_coef, 'gz', split_axis=0, concat_axis=0, tiled=True)  11.1 us
    all_to_all x1, starting transfers between devices, body(): back = lax.all_to_all(answer, 'gz', split_axis=0, concat_axis=0, tiled=True)  10.7 us
    all_to_all x1, waiting for transfers between devices, body(): back = lax.all_to_all(answer, 'gz', split_axis=0, concat_axis=0, tiled=True)  10 us
    all_to_all x1, starting transfers between devices, body(): lax.all_to_all(sent_coef, 'gz', split_axis=0, concat_axis=0, tiled=True)  8.38 us
    ppermute x4, starting transfers between devices, extended(): after = lax.ppermute(leading, axis, down)  7.19 us
    all_to_all x1, waiting for transfers between devices, body(): lax.all_to_all(sent_cell, 'gz', split_axis=0, concat_axis=0, tiled=True)  5.37 us
  transfers between devices with their start and end apart: 11, of which 8 were waited for; matrix products, arithmetic and copies ran while one was open for 7% of the time, Pallas kernels for 0%

commit v1 on v0

--- a/solution.py
+++ b/solution.py
@@ -1,9 +1,108 @@
 import jax
 import jax.numpy as jnp
 from jax import lax
+from jax.experimental import pallas as pl
+from jax.experimental.pallas import tpu as pltpu
 from jax.sharding import PartitionSpec as P
 
 STEPS = 2
+MESH = pl.DeviceIdType.MESH
+HIGHEST = lax.Precision.HIGHEST
+f32 = jnp.float32
+bf16 = jnp.bfloat16
+
+
+def hops(pair):
+    o, e = pair
+    return min(o, 8 - o) + min(e, 16 - e) / 2
+
+
+PEERS = sorted([(o, e) for o in range(8) for e in range(16) if (o, e) != (0, 0)], key=lambda p: -hops(p))
+
+
+def peer(z, d, o, e):
+    return lax.rem(z + o, 8) * 16 + lax.rem(d + e, 16)
+
+
+def greet_group(sem, z, d):
+    for o, e in PEERS:
+        pl.semaphore_signal(sem, inc=1, device_id={"gz": peer(z, d, o, e)}, device_id_type=MESH)
+
+
+def send_rows(src, dst, send, recv, z, d, sign):
+    for o, e in PEERS:
+        row = pl.ds(o * 16 + e, 1)
+        to = peer(z, d, o, e) if sign > 0 else peer(z, d, (8 - o) % 8, (16 - e) % 16)
+        pltpu.make_async_remote_copy(
+            src_ref=src.at[row],
+            dst_ref=dst.at[row],
+            send_sem=send,
+            recv_sem=recv,
+            device_id={"gz": to},
+            device_id_type=MESH,
+        ).start()
+
+
+def wait_rows(buf, sem):
+    rows = buf.at[pl.ds(1, 127)]
+    pltpu.make_async_copy(rows, rows, sem).wait()
+
+
+def iota(shape, dim):
+    return lax.broadcasted_iota(jnp.int32, shape, dim)
+
+
+def flat_row(ref):
+    return jnp.concatenate([ref[0:1, :], ref[1:2, :]], axis=1)
+
+
+def dot_t(a, b):
+    return lax.dot_general(a, b, (((1,), (1,)), ((), ())), precision=HIGHEST, preferred_element_type=f32)
+
+
+def dot(a, b):
+    return jnp.dot(a, b, precision=HIGHEST, preferred_element_type=f32)
+
+
+def request_table(own_ref, vox_ref, rad_ref, rate_ref, z, d):
+    own, vox = flat_row(own_ref), flat_row(vox_ref)
+    rad, rate = flat_row(rad_ref), flat_row(rate_ref)
+    coef = rate * rad * rad
+    rel = (((own >> 4) - z) & 7) * 16 + (((own & 15) - d) & 15)
+    named = (iota((128, 256), 0) == rel).astype(f32)
+    earlier = (iota((256, 256), 0) < iota((256, 256), 1)).astype(bf16)
+    before = jnp.dot(named.astype(bf16), earlier, preferred_element_type=f32)
+    rank = jnp.sum(before * named, axis=0, keepdims=True).astype(jnp.int32)
+    lane = iota((128, 256), 0)
+    value = jnp.where(lane < 4, coef, jnp.where(lane < 8, vox.astype(f32), 0.0))
+    value = jnp.where((lane & 3) == rank, value, 0.0)
+    return dot_t(named, value), named, rank, coef
+
+
+def serve(table, density):
+    rows = jnp.transpose(table)
+    coef = jnp.concatenate([rows[k : k + 1, :] for k in range(4)], axis=1)
+    code = jnp.concatenate([rows[k : k + 1, :] for k in range(4, 8)], axis=1).astype(jnp.int32)
+    hi = ((code >> 7) & 3) * 16 + (code >> 9)
+    lo = code & 127
+    at_hi = (iota((128, 512), 0) == hi).astype(f32)
+    at_lo = iota((128, 512), 0) == lo
+    field = jnp.concatenate([density[:, c * 128 : (c + 1) * 128] for c in range(4)] + [jnp.zeros((64, 128), f32)], axis=0)
+    picked = dot(jnp.transpose(field), at_hi)
+    rho = jnp.sum(jnp.where(at_lo, picked, 0.0), axis=0, keepdims=True)
+    answer = 2.0 - rho
+    spread = jnp.where(at_lo, 0.5 * coef * answer, 0.0)
+    total = dot_t(at_hi, spread)
+    source = jnp.concatenate([total[c * 16 : (c + 1) * 16, :] for c in range(4)], axis=1)
+    reply = jnp.concatenate([answer[:, k * 128 : (k + 1) * 128] for k in range(4)] + [jnp.zeros((124, 128), f32)], axis=0)
+    return jnp.transpose(reply), source
+
+
+def read_reply(reply, named, rank, coef):
+    rows = jnp.transpose(reply)[0:8, :]
+    got = dot(rows, named)
+    answer = jnp.sum(jnp.where(iota((8, 256), 0) == rank, got, 0.0), axis=0, keepdims=True)
+    return coef * answer
 
 
 VELOCITIES = [
@@ -32,6 +131,41 @@
 OMEGA = 1.6
 
 
+def density_of(pops):
+    near = pops[1]
+    for q in range(2, 7):
+        near = near + pops[q]
+    far = pops[7]
+    for q in range(8, 19):
+        far = far + pops[q]
+    return pops[0] * (1.0 / 3.0) + near * (1.0 / 18.0) + far * (1.0 / 36.0)
+
+
+def droplets(own, vox, rad, rate, pops, flux, source, ask, asked, tell, told, sends, recvs):
+    me = lax.axis_index("gz")
+    z, d = me // 16, lax.rem(me, 16)
+    barrier = pltpu.get_barrier_semaphore()
+    greet_group(barrier, z, d)
+    table, named, rank, coef = request_table(own, vox, rad, rate, z, d)
+    ask[...] = table
+    density = density_of([pops[q].astype(f32) for q in range(19)])
+    pl.semaphore_wait(barrier, 127)
+    send_rows(ask, asked, sends.at[0], recvs.at[0], z, d, 1)
+    asked[0:1, :] = ask[0:1, :]
+    wait_rows(asked, recvs.at[0])
+    reply, total = serve(asked[...], density)
+    tell[...] = reply
+    send_rows(tell, told, sends.at[1], recvs.at[1], z, d, -1)
+    told[0:1, :] = tell[0:1, :]
+    source[...] = total
+    wait_rows(told, recvs.at[1])
+    row = read_reply(told[...], named, rank, coef)
+    flux[0:1, :] = row[:, 0:128]
+    flux[1:2, :] = row[:, 128:256]
+    wait_rows(ask, sends.at[0])
+    wait_rows(tell, sends.at[1])
+
+
 def extended(array, sides, width):
     for axis, dim in sides:
         size, length = (lax.axis_size(axis), array.shape[dim])
@@ -84,32 +218,19 @@
 
 
 def body(populations, solid, radius, rate, ice_mass, owner, voxel):
-    planes, across, width = solid.shape
-    density0 = moments(populations.astype(jnp.float32))[0].reshape(-1)
-    coef = rate * radius * radius
-    owners = lax.axis_size("gz")
-    count = coef.shape[0]
-    accum = jnp.zeros((planes * across * width,), jnp.float32)
-    capacity = max(2, 2 * count // owners)
-    target = owner[:, 0]
-    onehot = (target[:, None] == jnp.arange(owners, dtype=jnp.int32)[None, :]).astype(jnp.int32)
-    before = jnp.cumsum(onehot, 0) - onehot
-    slot_rank = jnp.sum(before * onehot, 1)
-    position = target * capacity + slot_rank
-    sent_coef = jnp.zeros((owners * capacity,), jnp.float32).at[position].set(coef)
-    sent_cell = (
-        jnp.zeros((owners * capacity,), jnp.float32).at[position].set(voxel.astype(jnp.float32))
-    )
-    got_coef, got_cell = (
-        lax.all_to_all(sent_coef, "gz", split_axis=0, concat_axis=0, tiled=True),
-        lax.all_to_all(sent_cell, "gz", split_axis=0, concat_axis=0, tiled=True),
-    )
-    cells = got_cell.astype(jnp.int32)
-    answer = got_coef * (2.0 - density0[cells])
-    accum = accum.at[cells].add(0.5 * answer)
-    back = lax.all_to_all(answer, "gz", split_axis=0, concat_axis=0, tiled=True)
-    flux = back[position]
-    source = accum.reshape(planes, across, width).astype(jnp.bfloat16)
+    pops = populations.reshape(19, 16, 512)
+    vm = pl.BlockSpec(memory_space=pltpu.VMEM)
+    flux, source = pl.pallas_call(
+        droplets,
+        out_shape=(jax.ShapeDtypeStruct((2, 128), f32), jax.ShapeDtypeStruct((16, 512), f32)),
+        in_specs=[vm] * 5,
+        out_specs=(vm, vm),
+        scratch_shapes=[pltpu.VMEM((128, 128), f32)] * 4 + [pltpu.SemaphoreType.DMA((2,))] * 2,
+        name="droplets",
+        compiler_params=pltpu.CompilerParams(collective_id=0, has_side_effects=True, vmem_limit_bytes=32 * 2**20),
+    )(owner.reshape(2, 128), voxel.reshape(2, 128), radius.reshape(2, 128), rate.reshape(2, 128), pops)
+    flux = flux.reshape(-1)
+    source = source.reshape(solid.shape).astype(bf16)
     solid_flag = solid > 0
     state = populations
     for step in range(STEPS):

time: 132 us -> 89.8 us (0.68)
  the two profiles are of different devices: /device:TPU:1 before, /device:TPU:70 now
where the time goes in v1:
time: 89.8 us; the launch traced here: 89.3 us
  Pallas kernels  29 us (32%)
  waiting for transfers between devices  23.4 us (26%)
  starting transfers between devices  16.6 us (18%)
  local copies, waits for them, and re-layouts  11.9 us (13%)
  other arithmetic  3.85 us (4%)
  matrix products  3.3 us (4%)
  between operations  1.28 us (1%)
    pallas_call x1, Pallas kernels, body(): pl.pallas_call(droplets, out_shape=(jax.ShapeDtypeStruct((2, 128), f32),...  29 us
    ppermute x4, waiting for transfers between devices, extended(): before = lax.ppermute(last, axis, up)  20.4 us
    ppermute x4, starting transfers between devices, extended(): after = lax.ppermute(leading, axis, down)  9.45 us
    ppermute x4, starting transfers between devices, extended(): before = lax.ppermute(last, axis, up)  7.14 us
    unnamed x38, local copies, waits for them, and re-layouts  4.77 us
    ppermute x4, waiting for transfers between devices, extended(): after = lax.ppermute(leading, axis, down)  2.96 us
    dot_general x2, matrix products, collide(): jnp.tensordot(jnp.array(VELOCITIES, jnp.float32), velocity, axes=1, preci...  2.53 us
    another operation x22, local copies, waits for them, and re-layouts, stream(): return jnp.stack(moved)  2.37 us
  transfers between devices with their start and end apart: 8, of which 8 were waited for; matrix products, arithmetic and copies ran while one was open for 1% of the time, Pallas kernels for 0%

profile of v1, /device:TPU:70, one launch (start us, length us, event | category | flops | bytes accessed | tf_op | source)
XLA Modules:
  0.0 89.3 jit_solution(1738565834328528326)
XLA Ops:
  0.6 1.1 %copy.365 = bf16[19,2,8,512]{3,0,2,1:T(8,128)(2,1)S(1)} copy(bf16[19,2,8,512]{3,2,1,0:T(8,128)(2,1)} %param.11) | data formatting | bytes 622592 | tf_op args[0]
  1.8 0.7 fusion.23
  2.8 0.5 copy-done.1
  3.2 29.0 %droplets.1 = (f32[2,128]{1,0:T(2,128)S(1)}, f32[16,512]{1,0:T(8,128)S(1)}) custom-call(s32[2,128]{1,0:T(2,128)S(1)} %bitcast.129, s32[2,128]{1,0:T(2,128)S(1)} %bitcast.130, f32[2,128]{1,0:T(2,128)S(1)} %bitcast.131, f32[2,128]{1,0:T(2,128)S(1)} %bitcast.132, bf16[19,16,512]{2,1,0:T(8,128)(2,1)S(1)} %bitcast.127), custom_call_target="tpu_custom_call" | custom-call | tf_op jit(solution)/shard_map/droplets/pallas_call | solution.py:223
  32.2 0.7 copy-done.6
  32.9 0.5 fusion.18
  33.6 0.7 copy-done.5
  34.3 0.9 %stack.90 = bf16[19,2,8,512]{3,0,2,1:T(8,128)(2,1)S(1)} concatenate(bf16[1,2,8,512]{3,0,2,1:T(2,128)(2,1)S(1)} %get-tuple-element.106, bf16[1,2,8,512]{3,0,2,1:T(2,128)(2,1)S(1)} %get-tuple-element.105, bf16[1,2,8,512]{3,0,2,1:T(2,128)(2,1)S(1)} %get-tuple-element.104, bf16[1,2,8,512]{3,0,2,1:T(2,128)(2,1)S(1)} %get-tuple-element.103, ...), dimensions={0} | concatenate | bytes 622592 | tf_op jit(solution)/shard_map/stack | solution.py:204
  35.2 1.3 %fusion.8 = bf16[19,2,8,512]{3,0,2,1:T(8,128)(2,1)S(1)} fusion(bf16[19,2,8,512]{3,0,2,1:T(8,128)(2,1)S(1)} %stack.90, f32[19,3,1,1]{0,1,3,2:T(4,128)S(1)} %copy-done.8, f32[2,8,512]{2,1,0:T(8,128)S(1)} %bitcast_convert_fusion, f32[2,8,512]{2,1,0:T(8,128)S(1)} %broadcast_multiply_fusion.1, f32[2,8,512]{2,1,0:T(8,128)S(1)} %bitcast.136, ...), kind=kOutput, calls=%fused_computation.10 | convolution fusion | flops 7651328 | bytes 1288192 | tf_op jit(solution)/shard_map/dot_general | solution.py:198
  36.6 2.3 %collective-permute-start.1 = (bf16[19,1,8,512]{3,0,2,1:T(8,128)(2,1)S(1)}, bf16[19,1,8,512]{3,0,2,1:T(8,128)(2,1)S(1)}, u32[]{:S(2)}, u32[]{:S(2)}) collective-permute-start(bf16[19,1,8,512]{3,0,2,1:T(8,128)(2,1)S(1)} %get-tuple-element.86), channel_id=1, source_target_pairs={{4,0},{8,4},{12,8},{16,12},{20,16},{24,20},{28,24},{32,28},{36,32}... | collective-permute-start | bytes 466952 | tf_op jit(solution)/shard_map/ppermute | solution.py:177
  38.9 2.0 %collective-permute-start = (bf16[19,1,8,512]{3,0,2,1:T(8,128)(2,1)S(1)}, bf16[19,1,8,512]{3,0,2,1:T(8,128)(2,1)S(1)}, u32[]{:S(2)}, u32[]{:S(2)}) collective-permute-start(bf16[19,1,8,512]{3,0,2,1:T(8,128)(2,1)S(1)} %get-tuple-element.87), channel_id=1, source_target_pairs={{0,4},{4,8},{8,12},{12,16},{16,20},{20,24},{24,28},{28,32},{32,36}... | collective-permute-start | bytes 466952 | tf_op jit(solution)/shard_map/ppermute | solution.py:176
  40.9 1.2 %collective-permute-done.1 = bf16[19,1,8,512]{3,0,2,1:T(8,128)(2,1)S(1)} collective-permute-done((bf16[19,1,8,512]{3,0,2,1:T(8,128)(2,1)S(1)}, bf16[19,1,8,512]{3,0,2,1:T(8,128)(2,1)S(1)}, u32[]{:S(2)}, u32[]{:S(2)}) %collective-permute-start.1) | collective-permute-done | bytes 155680 | tf_op jit(solution)/shard_map/ppermute | solution.py:177
  42.1 5.9 %collective-permute-done = bf16[19,1,8,512]{3,0,2,1:T(8,128)(2,1)S(1)} collective-permute-done((bf16[19,1,8,512]{3,0,2,1:T(8,128)(2,1)S(1)}, bf16[19,1,8,512]{3,0,2,1:T(8,128)(2,1)S(1)}, u32[]{:S(2)}, u32[]{:S(2)}) %collective-permute-start) | collective-permute-done | bytes 155680 | tf_op jit(solution)/shard_map/ppermute | solution.py:176
  48.1 2.7 %collective-permute-start.3 = (bf16[19,4,1,512]{3,0,2,1:T(8,128)(2,1)S(1)}, bf16[19,4,1,512]{3,0,2,1:T(8,128)(2,1)S(1)}, u32[]{:S(2)}, u32[]{:S(2)}) collective-permute-start(bf16[19,4,1,512]{3,0,2,1:T(8,128)(2,1)S(1)} %get-tuple-element.41), channel_id=1, source_target_pairs={{1,0},{2,1},{3,2},{5,4},{6,5},{7,6},{9,8},{10,9},{11,10},{13,12},{... | collective-permute-start | bytes 233480 | tf_op jit(solution)/shard_map/ppermute | solution.py:177
  50.8 1.5 %collective-permute-start.2 = (bf16[19,4,1,512]{3,0,2,1:T(8,128)(2,1)S(1)}, bf16[19,4,1,512]{3,0,2,1:T(8,128)(2,1)S(1)}, u32[]{:S(2)}, u32[]{:S(2)}) collective-permute-start(bf16[19,4,1,512]{3,0,2,1:T(8,128)(2,1)S(1)} %get-tuple-element.42), channel_id=1, source_target_pairs={{0,1},{1,2},{2,3},{4,5},{5,6},{6,7},{8,9},{9,10},{10,11},{12,13},{... | collective-permute-start | bytes 233480 | tf_op jit(solution)/shard_map/ppermute | solution.py:176
  52.3 0.7 collective-permute-done.3
  53.3 4.0 %collective-permute-done.2 = bf16[19,4,1,512]{3,0,2,1:T(8,128)(2,1)S(1)} collective-permute-done((bf16[19,4,1,512]{3,0,2,1:T(8,128)(2,1)S(1)}, bf16[19,4,1,512]{3,0,2,1:T(8,128)(2,1)S(1)}, u32[]{:S(2)}, u32[]{:S(2)}) %collective-permute-start.2) | collective-permute-done | bytes 77856 | tf_op jit(solution)/shard_map/ppermute | solution.py:176
  59.7 0.9 %stack.101 = bf16[19,2,8,512]{3,0,2,1:T(8,128)(2,1)S(1)} concatenate(bf16[1,2,8,512]{3,0,2,1:T(2,128)(2,1)S(1)} %get-tuple-element.85, bf16[1,2,8,512]{3,0,2,1:T(2,128)(2,1)S(1)} %get-tuple-element.57, bf16[1,2,8,512]{3,0,2,1:T(2,128)(2,1)S(1)} %get-tuple-element.58, bf16[1,2,8,512]{3,0,2,1:T(2,128)(2,1)S(1)} %get-tuple-element.55, bf16[1,2,8,512]{3,0,2,1:T(2,128)(2,1)S(1)} %get-tuple-element.56, ...), dimensions={0} | concatenate | bytes 622592 | tf_op jit(solution)/shard_map/stack | solution.py:217
  60.6 0.6 fusion.21
  61.8 0.9 %stack.102 = bf16[19,2,8,512]{3,0,2,1:T(8,128)(2,1)S(1)} concatenate(bf16[1,2,8,512]{3,0,2,1:T(2,128)(2,1)S(1)} %get-tuple-element.82, bf16[1,2,8,512]{3,0,2,1:T(2,128)(2,1)S(1)} %get-tuple-element.81, bf16[1,2,8,512]{3,0,2,1:T(2,128)(2,1)S(1)} %get-tuple-element.80, bf16[1,2,8,512]{3,0,2,1:T(2,128)(2,1)S(1)} %get-tuple-element.79, bf16[1,2,8,512]{3,0,2,1:T(2,128)(2,1)S(1)} %get-tuple-element.78, ...), dimensions={0} | concatenate | bytes 622592 | tf_op jit(solution)/shard_map/stack | solution.py:204
  62.7 1.2 %fusion.17 = bf16[19,2,8,512]{3,0,2,1:T(8,128)(2,1)S(1)} fusion(bf16[19,2,8,512]{3,0,2,1:T(8,128)(2,1)S(1)} %stack.102, f32[19,3,1,1]{0,1,3,2:T(4,128)S(1)} %copy-done.8, f32[2,8,512]{2,1,0:T(8,128)S(1)} %broadcast_multiply_fusion, f32[2,8,512]{2,1,0:T(8,128)S(1)} %bitcast.134, f32[2,8,512]{2,1,0:T(8,128)S(1)} %bitcast_convert_fusion, ...), kind=kOutput, calls=%fused_computation.19 | convolution fusion | flops 7651328 | bytes 1370112 | tf_op jit(solution)/shard_map/dot_general | solution.py:198
  63.9 1.9 %collective-permute-start.5 = (bf16[19,1,8,512]{3,0,2,1:T(8,128)(2,1)S(1)}, bf16[19,1,8,512]{3,0,2,1:T(8,128)(2,1)S(1)}, u32[]{:S(2)}, u32[]{:S(2)}) collective-permute-start(bf16[19,1,8,512]{3,0,2,1:T(8,128)(2,1)S(1)} %get-tuple-element.62), channel_id=1, source_target_pairs={{4,0},{8,4},{12,8},{16,12},{20,16},{24,20},{28,24},{32,28},{36,32}... | collective-permute-start | bytes 466952 | tf_op jit(solution)/shard_map/ppermute | solution.py:177
  65.9 2.4 %collective-permute-start.4 = (bf16[19,1,8,512]{3,0,2,1:T(8,128)(2,1)S(1)}, bf16[19,1,8,512]{3,0,2,1:T(8,128)(2,1)S(1)}, u32[]{:S(2)}, u32[]{:S(2)}) collective-permute-start(bf16[19,1,8,512]{3,0,2,1:T(8,128)(2,1)S(1)} %get-tuple-element.63), channel_id=1, source_target_pairs={{0,4},{4,8},{8,12},{12,16},{16,20},{20,24},{24,28},{28,32},{32,36}... | collective-permute-start | bytes 466952 | tf_op jit(solution)/shard_map/ppermute | solution.py:176
  68.3 0.8 collective-permute-done.5
  69.0 5.9 %collective-permute-done.4 = bf16[19,1,8,512]{3,0,2,1:T(8,128)(2,1)S(1)} collective-permute-done((bf16[19,1,8,512]{3,0,2,1:T(8,128)(2,1)S(1)}, bf16[19,1,8,512]{3,0,2,1:T(8,128)(2,1)S(1)}, u32[]{:S(2)}, u32[]{:S(2)}) %collective-permute-start.4) | collective-permute-done | bytes 155680 | tf_op jit(solution)/shard_map/ppermute | solution.py:176
  75.0 2.4 %collective-permute-start.7 = (bf16[19,4,1,512]{3,0,2,1:T(8,128)(2,1)S(1)}, bf16[19,4,1,512]{3,0,2,1:T(8,128)(2,1)S(1)}, u32[]{:S(2)}, u32[]{:S(2)}) collective-permute-start(bf16[19,4,1,512]{3,0,2,1:T(8,128)(2,1)S(1)} %get-tuple-element.37), channel_id=1, source_target_pairs={{1,0},{2,1},{3,2},{5,4},{6,5},{7,6},{9,8},{10,9},{11,10},{13,12},{... | collective-permute-start | bytes 233480 | tf_op jit(solution)/shard_map/ppermute | solution.py:177
  77.5 0.6 bitcast_subtract_fusion
  78.0 1.3 %collective-permute-start.6 = (bf16[19,4,1,512]{3,0,2,1:T(8,128)(2,1)S(1)}, bf16[19,4,1,512]{3,0,2,1:T(8,128)(2,1)S(1)}, u32[]{:S(2)}, u32[]{:S(2)}) collective-permute-start(bf16[19,4,1,512]{3,0,2,1:T(8,128)(2,1)S(1)} %get-tuple-element.38), channel_id=1, source_target_pairs={{0,1},{1,2},{2,3},{4,5},{5,6},{6,7},{8,9},{9,10},{10,11},{12,13},{... | collective-permute-start | bytes 233480 | tf_op jit(solution)/shard_map/ppermute | solution.py:176
  80.0 4.6 %collective-permute-done.6 = bf16[19,4,1,512]{3,0,2,1:T(8,128)(2,1)S(1)} collective-permute-done((bf16[19,4,1,512]{3,0,2,1:T(8,128)(2,1)S(1)}, bf16[19,4,1,512]{3,0,2,1:T(8,128)(2,1)S(1)}, u32[]{:S(2)}, u32[]{:S(2)}) %collective-permute-start.6) | collective-permute-done | bytes 77856 | tf_op jit(solution)/shard_map/ppermute | solution.py:176
  87.0 0.9 %stack.113 = bf16[19,2,8,512]{3,0,2,1:T(8,128)(2,1)S(1)} concatenate(bf16[1,2,8,512]{3,0,2,1:T(2,128)(2,1)S(1)} %get-tuple-element.61, bf16[1,2,8,512]{3,0,2,1:T(2,128)(2,1)S(1)} %get-tuple-element.49, bf16[1,2,8,512]{3,0,2,1:T(2,128)(2,1)S(1)} %get-tuple-element.50, bf16[1,2,8,512]{3,0,2,1:T(2,128)(2,1)S(1)} %get-tuple-element.47, bf16[1,2,8,512]{3,0,2,1:T(2,128)(2,1)S(1)} %get-tuple-element.48, ...), dimensions={0} | concatenate | bytes 622592 | tf_op jit(solution)/shard_map/stack | solution.py:217
  87.9 0.8 copy.313
  88.7 0.6 copy.379
  (122 shorter events, 6.5 us)
Async XLA Ops:
  1.8 1.0 %copy-start = (bf16[19,2,8,512]{3,2,1,0:T(8,128)(2,1)S(1)}, bf16[19,2,8,512]{3,2,1,0:T(8,128)(2,1)}, u32[]{:S(2)}) copy-start(bf16[19,2,8,512]{3,2,1,0:T(8,128)(2,1)} %param.11) | copy-start | bytes 933892
  1.8 1.0 %copy-start.2 = (s32[256]{0:T(256)S(1)}, s32[256]{0:T(256)}, u32[]{:S(2)}) copy-start(s32[256]{0:T(256)} %param.17) | copy-start | bytes 3076
  1.8 1.0 %copy-start.3 = (f32[256]{0:T(256)S(1)}, f32[256]{0:T(256)}, u32[]{:S(2)}) copy-start(f32[256]{0:T(256)} %param.13) | copy-start | bytes 3076
  1.8 0.9 %copy-start.4 = (f32[256]{0:T(256)S(1)}, f32[256]{0:T(256)}, u32[]{:S(2)}) copy-start(f32[256]{0:T(256)} %param.14) | copy-start | bytes 3076
  2.5 0.7 copy-start.1
  32.2 0.7 copy-start.6
  33.5 0.8 copy-start.5
  34.3 0.9 %copy-start.8 = (f32[19,3,1,1]{0,1,3,2:T(4,128)S(1)}, f32[19,3,1,1]{0,1,3,2:T(4,128)}, u32[]{:S(2)}) copy-start(f32[19,3,1,1]{0,1,3,2:T(4,128)} %constant.28) | copy-start | bytes 688
  36.6 5.5 %collective-permute-start.1 = (bf16[19,1,8,512]{3,0,2,1:T(8,128)(2,1)S(1)}, bf16[19,1,8,512]{3,0,2,1:T(8,128)(2,1)S(1)}, u32[]{:S(2)}, u32[]{:S(2)}) collective-permute-start(bf16[19,1,8,512]{3,0,2,1:T(8,128)(2,1)S(1)} %get-tuple-element.86), channel_id=1, source_target_pairs={{4,0},{8,4},{12,8},{16,12},{20,16},{24,20},{28,24},{32,28},{36,32}... | collective-permute-start | bytes 466952 | tf_op jit(solution)/shard_map/ppermute | solution.py:177
  38.9 9.1 %collective-permute-start = (bf16[19,1,8,512]{3,0,2,1:T(8,128)(2,1)S(1)}, bf16[19,1,8,512]{3,0,2,1:T(8,128)(2,1)S(1)}, u32[]{:S(2)}, u32[]{:S(2)}) collective-permute-start(bf16[19,1,8,512]{3,0,2,1:T(8,128)(2,1)S(1)} %get-tuple-element.87), channel_id=1, source_target_pairs={{0,4},{4,8},{8,12},{12,16},{16,20},{20,24},{24,28},{28,32},{32,36}... | collective-permute-start | bytes 466952 | tf_op jit(solution)/shard_map/ppermute | solution.py:176
  48.1 4.9 %collective-permute-start.3 = (bf16[19,4,1,512]{3,0,2,1:T(8,128)(2,1)S(1)}, bf16[19,4,1,512]{3,0,2,1:T(8,128)(2,1)S(1)}, u32[]{:S(2)}, u32[]{:S(2)}) collective-permute-start(bf16[19,4,1,512]{3,0,2,1:T(8,128)(2,1)S(1)} %get-tuple-element.41), channel_id=1, source_target_pairs={{1,0},{2,1},{3,2},{5,4},{6,5},{7,6},{9,8},{10,9},{11,10},{13,12},{... | collective-permute-start | bytes 233480 | tf_op jit(solution)/shard_map/ppermute | solution.py:177
  50.8 6.5 %collective-permute-start.2 = (bf16[19,4,1,512]{3,0,2,1:T(8,128)(2,1)S(1)}, bf16[19,4,1,512]{3,0,2,1:T(8,128)(2,1)S(1)}, u32[]{:S(2)}, u32[]{:S(2)}) collective-permute-start(bf16[19,4,1,512]{3,0,2,1:T(8,128)(2,1)S(1)} %get-tuple-element.42), channel_id=1, source_target_pairs={{0,1},{1,2},{2,3},{4,5},{5,6},{6,7},{8,9},{9,10},{10,11},{12,13},{... | collective-permute-start | bytes 233480 | tf_op jit(solution)/shard_map/ppermute | solution.py:176
  63.9 5.1 %collective-permute-start.5 = (bf16[19,1,8,512]{3,0,2,1:T(8,128)(2,1)S(1)}, bf16[19,1,8,512]{3,0,2,1:T(8,128)(2,1)S(1)}, u32[]{:S(2)}, u32[]{:S(2)}) collective-permute-start(bf16[19,1,8,512]{3,0,2,1:T(8,128)(2,1)S(1)} %get-tuple-element.62), channel_id=1, source_target_pairs={{4,0},{8,4},{12,8},{16,12},{20,16},{24,20},{28,24},{32,28},{36,32}... | collective-permute-start | bytes 466952 | tf_op jit(solution)/shard_map/ppermute | solution.py:177
  65.9 9.1 %collective-permute-start.4 = (bf16[19,1,8,512]{3,0,2,1:T(8,128)(2,1)S(1)}, bf16[19,1,8,512]{3,0,2,1:T(8,128)(2,1)S(1)}, u32[]{:S(2)}, u32[]{:S(2)}) collective-permute-start(bf16[19,1,8,512]{3,0,2,1:T(8,128)(2,1)S(1)} %get-tuple-element.63), channel_id=1, source_target_pairs={{0,4},{4,8},{8,12},{12,16},{16,20},{20,24},{24,28},{28,32},{32,36}... | collective-permute-start | bytes 466952 | tf_op jit(solution)/shard_map/ppermute | solution.py:176
  75.0 2.5 %copy-start.7 = (f32[256]{0:T(256)S(1)}, f32[256]{0:T(256)}, u32[]{:S(2)}) copy-start(f32[256]{0:T(256)} %param.15) | copy-start | bytes 3076
  75.0 4.6 %collective-permute-start.7 = (bf16[19,4,1,512]{3,0,2,1:T(8,128)(2,1)S(1)}, bf16[19,4,1,512]{3,0,2,1:T(8,128)(2,1)S(1)}, u32[]{:S(2)}, u32[]{:S(2)}) collective-permute-start(bf16[19,4,1,512]{3,0,2,1:T(8,128)(2,1)S(1)} %get-tuple-element.37), channel_id=1, source_target_pairs={{1,0},{2,1},{3,2},{5,4},{6,5},{7,6},{9,8},{10,9},{11,10},{13,12},{... | collective-permute-start | bytes 233480 | tf_op jit(solution)/shard_map/ppermute | solution.py:177
  78.0 6.5 %collective-permute-start.6 = (bf16[19,4,1,512]{3,0,2,1:T(8,128)(2,1)S(1)}, bf16[19,4,1,512]{3,0,2,1:T(8,128)(2,1)S(1)}, u32[]{:S(2)}, u32[]{:S(2)}) collective-permute-start(bf16[19,4,1,512]{3,0,2,1:T(8,128)(2,1)S(1)} %get-tuple-element.38), channel_id=1, source_target_pairs={{0,1},{1,2},{2,3},{4,5},{5,6},{6,7},{8,9},{9,10},{10,11},{12,13},{... | collective-permute-start | bytes 233480 | tf_op jit(solution)/shard_map/ppermute | solution.py:176

commit v2 on v1

v2 whole, which is shorter than its diff:
```python
import jax
import jax.numpy as jnp
from jax import lax
from jax.experimental import pallas as pl
from jax.experimental.pallas import tpu as pltpu
from jax.sharding import PartitionSpec as P

MESH = pl.DeviceIdType.MESH
HIGHEST = lax.Precision.HIGHEST
f32 = jnp.float32
bf16 = jnp.bfloat16


def hops(pair):
    o, e = pair
    return min(o, 8 - o) + min(e, 16 - e) / 2


PEERS = sorted([(o, e) for o in range(8) for e in range(16) if (o, e) != (0, 0)], key=lambda p: -hops(p))


def peer(z, d, o, e):
    return lax.rem(z + o, 8) * 16 + lax.rem(d + e, 16)


def greet_group(sem, z, d):
    for o, e in PEERS:
        pl.semaphore_signal(sem, inc=1, device_id={"gz": peer(z, d, o, e)}, device_id_type=MESH)


def send_rows(src, dst, send, recv, z, d, sign):
    for o, e in PEERS:
        row = pl.ds(o * 16 + e, 1)
        to = peer(z, d, o, e) if sign > 0 else peer(z, d, (8 - o) % 8, (16 - e) % 16)
        pltpu.make_async_remote_copy(
            src_ref=src.at[row],
            dst_ref=dst.at[row],
            send_sem=send,
            recv_sem=recv,
            device_id={"gz": to},
            device_id_type=MESH,
        ).start()


def wait_rows(buf, sem):
    rows = buf.at[pl.ds(1, 127)]
    pltpu.make_async_copy(rows, rows, sem).wait()


def iota(shape, dim):
    return lax.broadcasted_iota(jnp.int32, shape, dim)


def flat_row(ref):
    return jnp.concatenate([ref[0:1, :], ref[1:2, :]], axis=1)


def dot_t(a, b):
    return lax.dot_general(a, b, (((1,), (1,)), ((), ())), precision=HIGHEST, preferred_element_type=f32)


def dot(a, b):
    return jnp.dot(a, b, precision=HIGHEST, preferred_element_type=f32)


def request_table(own_ref, vox_ref, rad_ref, rate_ref, z, d):
    own, vox = flat_row(own_ref), flat_row(vox_ref)
    rad, rate = flat_row(rad_ref), flat_row(rate_ref)
    coef = rate * rad * rad
    rel = (((own >> 4) - z) & 7) * 16 + (((own & 15) - d) & 15)
    named = (iota((128, 256), 0) == rel).astype(f32)
    earlier = (iota((256, 256), 0) < iota((256, 256), 1)).astype(bf16)
    before = jnp.dot(named.astype(bf16), earlier, preferred_element_type=f32)
    rank = jnp.sum(before * named, axis=0, keepdims=True).astype(jnp.int32)
    lane = iota((128, 256), 0)
    value = jnp.where(lane < 4, coef, jnp.where(lane < 8, vox.astype(f32), 0.0))
    value = jnp.where((lane & 3) == rank, value, 0.0)
    return dot_t(named, value), named, rank, coef


def serve(table, density):
    rows = jnp.transpose(table)
    coef = jnp.concatenate([rows[k : k + 1, :] for k in range(4)], axis=1)
    code = jnp.concatenate([rows[k : k + 1, :] for k in range(4, 8)], axis=1).astype(jnp.int32)
    hi = ((code >> 7) & 3) * 16 + (code >> 9)
    lo = code & 127
    at_hi = (iota((128, 512), 0) == hi).astype(f32)
    at_lo = iota((128, 512), 0) == lo
    field = jnp.concatenate([density[:, c * 128 : (c + 1) * 128] for c in range(4)] + [jnp.zeros((64, 128), f32)], axis=0)
    picked = dot(jnp.transpose(field), at_hi)
    rho = jnp.sum(jnp.where(at_lo, picked, 0.0), axis=0, keepdims=True)
    answer = 2.0 - rho
    spread = jnp.where(at_lo, 0.5 * coef * answer, 0.0)
    total = dot_t(at_hi, spread)
    source = jnp.concatenate([total[c * 16 : (c + 1) * 16, :] for c in range(4)], axis=1)
    reply = jnp.concatenate([answer[:, k * 128 : (k + 1) * 128] for k in range(4)] + [jnp.zeros((124, 128), f32)], axis=0)
    return jnp.transpose(reply), source


def read_reply(reply, named, rank):
    rows = jnp.transpose(reply)[0:8, :]
    got = dot(rows, named)
    return jnp.sum(jnp.where(iota((8, 256), 0) == rank, got, 0.0), axis=0, keepdims=True)


VELOCITIES = [
    (0, 0, 0),
    (1, 0, 0),
    (-1, 0, 0),
    (0, 1, 0),
    (0, -1, 0),
    (0, 0, 1),
    (0, 0, -1),
    (1, 1, 0),
    (-1, -1, 0),
    (1, -1, 0),
    (-1, 1, 0),
    (1, 0, 1),
    (-1, 0, -1),
    (1, 0, -1),
    (-1, 0, 1),
    (0, 1, 1),
    (0, -1, -1),
    (0, 1, -1),
    (0, -1, 1),
    (0, 0, 0),
]
FLAG = 19
UP = [q for q in range(19) if VELOCITIES[q][0] == 1]
FLAT = [q for q in range(20) if VELOCITIES[q][0] == 0]
DOWN = [q for q in range(19) if VELOCITIES[q][0] == -1]
ZPLACE = {q: i for i, q in enumerate(UP + FLAT + DOWN)}
XUP = [q for q in range(19) if VELOCITIES[q][1] == 1]
XFLAT = [q for q in range(20) if VELOCITIES[q][1] == 0]
XDOWN = [q for q in range(19) if VELOCITIES[q][1] == -1]
XTILES = XUP + XUP[-1:] + XFLAT + XDOWN + XDOWN[-1:]
XPLACE = {q: XTILES.index(q) for q in range(20)}
NEAR = [(a, b) for a in (-1, 0, 1) for b in (-1, 0, 1) if (a, b) != (0, 0)]
ASIDE = [(a, b) for a, b in NEAR if b != 0]


def dotc(c, v):
    total = None
    for k, x in zip(c, v):
        if k:
            total = (x if k > 0 else -x) if total is None else (total + x if k > 0 else total - x)
    return total


def total_of(terms):
    out = terms[0]
    for t in terms[1:]:
        out = out + t
    return out


def density_of(g):
    near = total_of([g[q] for q in range(1, 7)])
    far = total_of([g[q] for q in range(7, 19)])
    return g[0] * (1.0 / 3.0) + near * (1.0 / 18.0) + far * (1.0 / 36.0)


def collide(g, solid, source, wanted):
    diff = {q: g[q] - g[q + 1] for q in range(1, 19, 2)}
    rho = density_of(g)
    j = []
    for axis in range(3):
        far = None
        for q in range(7, 19, 2):
            k = VELOCITIES[q][axis]
            if k:
                far = diff[q] if far is None else (far + diff[q] if k > 0 else far - diff[q])
        j.append(diff[1 + 2 * axis] * (4.8 / 18.0) + far * (4.8 / 36.0))
    scale = (1.5 / 4.8) / rho
    u = [x * scale for x in j]
    own = [x * y for x, y in zip(j, u)]
    base = 1.6 * rho - (own[0] + own[1] + own[2]) * (1.0 / 3.0)
    if source is not None:
        base = base + source
    out = {}
    if 0 in wanted:
        out[0] = jnp.where(solid, g[0], base - 0.6 * g[0])
    for q in range(1, 19, 2):
        if q not in wanted and q + 1 not in wanted:
            continue
        odd = dotc(VELOCITIES[q], j)
        even = base + (own[q // 2] if q < 7 else odd * dotc(VELOCITIES[q], u))
        if q in wanted:
            out[q] = jnp.where(solid, g[q + 1], even + odd - 0.6 * g[q])
        if q + 1 in wanted:
            out[q + 1] = jnp.where(solid, g[q], even - odd - 0.6 * g[q + 1])
    return out, rho


def wide(ref, q, rows):
    return jnp.concatenate([ref[q, c, rows, :] for c in range(4)], axis=1)


def put(ref, q, rows, value):
    for c in range(4):
        ref[q, c, rows, :] = value[:, 128 * c : 128 * c + 128]


def lane_roll(x, cy):
    return x if cy == 0 else pltpu.roll(x, cy % 512, 1)


def row_roll(x, k):
    return pltpu.roll(x, k % x.shape[0], 0)


def remote(src, dst, send, recv, gz, col):
    return pltpu.make_async_remote_copy(
        src_ref=src, dst_ref=dst, send_sem=send, recv_sem=recv, device_id={"gz": gz, "col": col}, device_id_type=MESH
    )


def step_pair(own, vox, rad, rate, solid, pops, out, answer, *scratch):
    (own_v, vox_v, rad_v, rate_v, solid_v, pops_v, ask, asked, tell, told, rel, below, above, edge, left, right) = scratch[:16]
    (src, near, spread, work, post, dens, loads, sends, recvs, zsend, zrecv, xsend, xrecv, nsend, nrecv) = scratch[16:]
    gz, col = lax.axis_index("gz"), lax.axis_index("col")
    z, d = gz // 16, lax.rem(gz, 16)
    barrier = pltpu.get_barrier_semaphore()

    fetch = [
        pltpu.make_async_copy(a, b, loads.at[i])
        for i, (a, b) in enumerate(
            [(own, own_v), (vox, vox_v), (rad, rad_v), (rate, rate_v), (solid, solid_v), (pops, pops_v)]
        )
    ]
    for c in fetch:
        c.start()
    greet_group(barrier, z, d)

    def beside(dz, dx):
        return lax.rem(gz + dz + 128, 128), lax.rem(col + dx + 4, 4)

    for dz, dx in ASIDE:
        g, c = beside(dz, dx)
        pl.semaphore_signal(barrier, inc=1, device_id={"gz": g, "col": c}, device_id_type=MESH)
    for c in fetch:
        c.wait()
    table, named, rank, coef = request_table(own_v, vox_v, rad_v, rate_v, z, d)
    ask[...] = table

    def first(i, carry):
        lanes = pl.ds(pl.multiple_of(i * 128, 128), 128)
        g = [pops_v[q, :, lanes].astype(f32) for q in range(19)]
        made, rho = collide(g, solid_v[:, lanes] > 0, None, range(19))
        dens[:, lanes] = rho
        for q in range(19):
            post[q, i, 0:16, :] = made[q]
        return carry

    lax.fori_loop(0, 4, first, 0)
    for q in range(19):
        rel[ZPLACE[q]] = lane_roll(wide(post, q, pl.ds(0, 16)), VELOCITIES[q][2]).astype(bf16)
    rel[ZPLACE[FLAG]] = jnp.where(solid_v[...] > 0, 1.0, 0.0).astype(bf16)

    pl.semaphore_wait(barrier, 127 + len(ASIDE))
    up, down = beside(1, 0), beside(-1, 0)
    zcopies = [
        remote(rel.at[pl.ds(0, 15)], below, zsend.at[0], zrecv.at[0], *up),
        remote(rel.at[pl.ds(5, 15)], above, zsend.at[1], zrecv.at[1], *down),
    ]
    for c in zcopies:
        c.start()
    send_rows(ask, asked, sends.at[0], recvs.at[0], z, d, 1)
    asked[0:1, :] = ask[0:1, :]

    for c in zcopies:
        c.wait_recv()
    has_below, has_above = gz > 0, gz < 127
    for q in range(20):
        cz, i = VELOCITIES[q][0], ZPLACE[q]
        mine = rel[i].astype(f32)
        if cz >= 0:
            under = jnp.where(has_below, below[i].astype(f32), 0.0)
        if cz <= 0:
            over = jnp.where(has_above, above[i - 5].astype(f32), 0.0)
        if cz == 1:
            rows = [under, mine]
        elif cz == -1:
            rows = [mine, over]
        else:
            rows = [under[8:16], mine, over[0:8]]
        put(work, q, pl.ds(0, 32), jnp.concatenate(rows, axis=0))

    def column(q, x):
        return wide(work, q, pl.ds(x, 4, stride=8))

    def edge_tile(q):
        cx = VELOCITIES[q][1]
        first_x, then_x = {0: (7, 0), 1: (7, 6), -1: (0, 1)}[cx]
        return jnp.concatenate([column(q, first_x), column(q, then_x)], axis=0)

    for b in range(11):
        edge[b] = jnp.concatenate([edge_tile(XTILES[2 * b]), edge_tile(XTILES[2 * b + 1])], axis=0).astype(bf16)
    to_right, to_left = beside(0, 1), beside(0, -1)
    xcopies = [
        remote(edge.at[pl.ds(0, 8)], left, xsend.at[0], xrecv.at[0], *to_right),
        remote(edge.at[pl.ds(3, 8)], right, xsend.at[1], xrecv.at[1], *to_left),
    ]
    for c in xcopies:
        c.start()

    wait_rows(asked, recvs.at[0])
    reply, total = serve(asked[...], dens[...])
    src[...] = jnp.where(solid_v[...] > 0, 0.0, total).astype(bf16)
    ncopies = []
    for i, (dz, dx) in enumerate(NEAR):
        ncopies.append(remote(src, near.at[7 - i], nsend.at[i], nrecv.at[7 - i], *beside(dz, dx)))
    for c in ncopies:
        c.start()
    tell[...] = reply
    send_rows(tell, told, sends.at[1], recvs.at[1], z, d, -1)
    told[0:1, :] = tell[0:1, :]

    for c in xcopies:
        c.wait_recv()
    has_left, has_right = col > 0, col < 3
    row8 = iota((8, 512), 0)

    def tile(ref, shift, q, there):
        k = XPLACE[q] - shift
        both = jnp.where(there, ref[k // 2].astype(f32), 0.0)
        return both[8 * (k % 2) : 8 * (k % 2) + 8]

    for q in range(20):
        cx = VELOCITIES[q][1]
        if cx == 0:
            put(work, q, pl.ds(32, 8), jnp.where(row8 < 4, tile(left, 0, q, has_left), tile(right, 6, q, has_right)))
        else:
            ends = tile(left, 0, q, has_left) if cx == 1 else tile(right, 6, q, has_right)
            k = XPLACE[q]
            mine = edge[k // 2].astype(f32)[8 * (k % 2) : 8 * (k % 2) + 8]
            merged = jnp.where(row8 < 4, mine, ends)
            put(work, q, pl.ds(32, 8), row_roll(merged, 4) if cx == 1 else merged)
            put(work, q, pl.ds(0, 32), row_roll(wide(work, q, pl.ds(0, 32)), cx))
            put(work, q, pl.ds(0 if cx == 1 else 7, 4, stride=8), ends[0:4])

    for i in range(8):
        remote(src, near.at[i], nsend.at[7 - i], nrecv.at[i], gz, col).wait_recv()
    for a in (-1, 0, 1):
        for b in (-1, 0, 1):
            there = True
            if (a, b) == (0, 0):
                block = src[...].astype(f32)
            else:
                block = near[NEAR.index((a, b))].astype(f32)
                if a:
                    there = has_below if a < 0 else has_above
                if b:
                    sideways = has_left if b < 0 else has_right
                    there = jnp.logical_and(there, sideways) if a else sideways
                block = jnp.where(there, block, 0.0)
            for k in (0, 1):
                plane = block[8 * k : 8 * k + 8]
                at = 16 * (2 * (a + 1) + k)
                for cy in (-1, 0, 1):
                    moved = lane_roll(plane, cy)
                    if b == 0:
                        put(spread, cy + 1, pl.ds(at + 2, 8), moved)
                    elif b < 0:
                        put(spread, cy + 1, pl.ds(at, 2), moved[6:8])
                    else:
                        put(spread, cy + 1, pl.ds(at + 10, 2), moved[0:2])
    for q in range(20):
        cz, cx, cy = VELOCITIES[q]
        rows = [pl.ds(16 * (p + 1 - cz) + 2 - cx, 8) for p in range(4)]
        rows += [pl.ds(16 * (1 - cz) + k - cx, 4, stride=16) for k in (1, 10)]
        for c in range(4):
            added = jnp.concatenate([spread[cy + 1, c, r, :] for r in rows], axis=0)
            if q == FLAG:
                post[FLAG, c] = added
            else:
                work[q, c] = (work[q, c] + added).astype(bf16).astype(f32)

    row = iota((8, 128), 0)
    plane_in = jnp.logical_and(
        jnp.logical_or((row & 3) != 0, has_below), jnp.logical_or((row & 3) != 3, has_above)
    )
    side_in = jnp.logical_or(jnp.logical_and(row < 4, has_left), jnp.logical_and(row >= 4, has_right))
    edge_in = jnp.logical_and(plane_in, side_in)
    jobs = [(8, range(19), None), (16, range(19), None), (0, UP, has_below), (24, DOWN, has_above), (32, XUP + XDOWN, edge_in)]

    def second(i, carry):
        for r, wanted, inside in jobs:
            rows = pl.ds(r, 8)
            g = [work[q, i, rows, :] for q in range(19)]
            made, _ = collide(g, work[FLAG, i, rows, :] > 0.5, post[FLAG, i, rows, :], wanted)
            for q in wanted:
                post[q, i, rows, :] = made[q] if inside is None else jnp.where(inside, made[q], 0.0)
        return carry

    lax.fori_loop(0, 4, second, 0)
    for q in range(19):
        cz, cx, cy = VELOCITIES[q]
        r = 8 * (1 - cz)
        moved = wide(post, q, pl.ds(r, 16))
        if cx:
            moved = row_roll(moved, cx)
            rim = 32 + (1 - cz) if cx == 1 else 36 + (1 - cz)
            for k in (0, 1):
                at = 8 * k + (0 if cx == 1 else 7)
                moved = jnp.where(iota((16, 512), 0) == at, wide(post, q, pl.ds(rim + k, 1)), moved)
        out[q] = lane_roll(moved, cy).astype(bf16)

    wait_rows(told, recvs.at[1])
    line = read_reply(told[...], named, rank)
    answer[0:1, :] = line[:, 0:128]
    answer[1:2, :] = line[:, 128:256]
    wait_rows(ask, sends.at[0])
    wait_rows(tell, sends.at[1])
    for c in zcopies + xcopies + ncopies:
        c.wait_send()


def body(populations, solid, radius, rate, ice_mass, owner, voxel):
    vm = pl.BlockSpec(memory_space=pltpu.VMEM)
    anywhere = pl.BlockSpec(memory_space=pl.ANY)
    sem = pltpu.SemaphoreType.DMA
    small = [pltpu.VMEM((2, 128), jnp.int32)] * 2 + [pltpu.VMEM((2, 128), f32)] * 2
    state, answer = pl.pallas_call(
        step_pair,
        out_shape=(jax.ShapeDtypeStruct((19, 16, 512), bf16), jax.ShapeDtypeStruct((2, 128), f32)),
        in_specs=[anywhere] * 6,
        out_specs=(vm, vm),
        scratch_shapes=small
        + [pltpu.VMEM((16, 512), jnp.int32), pltpu.VMEM((19, 16, 512), bf16)]
        + [pltpu.VMEM((128, 128), f32)] * 4
        + [pltpu.VMEM((20, 16, 512), bf16)]
        + [pltpu.VMEM((15, 16, 512), bf16)] * 2
        + [pltpu.VMEM((11, 16, 512), bf16)]
        + [pltpu.VMEM((8, 16, 512), bf16)] * 2
        + [pltpu.VMEM((16, 512), bf16), pltpu.VMEM((8, 16, 512), bf16)]
        + [pltpu.VMEM((3, 4, 96, 128), f32)]
        + [pltpu.VMEM((20, 4, 40, 128), f32)] * 2
        + [pltpu.VMEM((16, 512), f32)]
        + [sem((6,))]
        + [sem((2,))] * 6
        + [sem((8,))] * 2,
        name="two_steps",
        compiler_params=pltpu.CompilerParams(collective_id=0, has_side_effects=True, vmem_limit_bytes=48 * 2**20),
    )(
        owner.reshape(2, 128),
        voxel.reshape(2, 128),
        radius.reshape(2, 128),
        rate.reshape(2, 128),
        solid.reshape(16, 512),
        populations.reshape(19, 16, 512),
    )
    flux = rate * radius * radius * answer.reshape(-1)
    return (state.reshape(populations.shape), flux, ice_mass - flux)


def solution(mesh):
    return jax.shard_map(
        body,
        mesh=mesh,
        in_specs=(
            P(None, "gz", "col", None),
            P("gz", "col", None),
            P(("gz", "col")),
            P(("gz", "col")),
            P(("gz", "col")),
            P(("gz", "col"), None),
            P(("gz", "col")),
        ),
        out_specs=(P(None, "gz", "col", None), P(("gz", "col")), P(("gz", "col"))),
        check_vma=False,
    )
```

time: 89.8 us -> 40.1 us (0.45)
  the two profiles are of different devices: /device:TPU:70 before, /device:TPU:1 now
where the time goes in v2:
time: 40.1 us; the launch traced here: 39.8 us
  Pallas kernels  34.7 us (87%)
  local copies, waits for them, and re-layouts  3.81 us (10%)
  between operations  0.68 us (2%)
  other arithmetic  0.57 us (1%)
    pallas_call x1, Pallas kernels, body(): pl.pallas_call(step_pair, out_shape=(jax.ShapeDtypeStruct((19, 16, 512),...  34.7 us
    unnamed x15, local copies, waits for them, and re-layouts  3.81 us

profile of v2, /device:TPU:1, one launch (start us, length us, event | category | flops | bytes accessed | tf_op | source)
XLA Modules:
  0.0 39.8 jit_solution(3405812958166092198)
XLA Ops:
  0.6 0.0 copy-start.5
  0.6 0.0 copy-start.3
  0.7 0.0 copy-start.4
  0.7 0.0 copy-start.2
  0.7 0.6 %copy-done.5 = s32[256]{0:T(256)S(1)} copy-done((s32[256]{0:T(256)S(1)}, s32[256]{0:T(256)}, u32[]{:S(2)}) %copy-start.5) | copy-done | bytes 1048
  1.3 0.0 copy-done.3
  1.3 0.0 copy-done.4
  1.3 0.0 copy-done.2
  1.4 0.0 copy-start
  1.4 1.0 %copy-done = bf16[19,2,8,512]{3,2,1,0:T(8,128)(2,1)S(1)} copy-done((bf16[19,2,8,512]{3,2,1,0:T(8,128)(2,1)S(1)}, bf16[19,2,8,512]{3,2,1,0:T(8,128)(2,1)}, u32[]{:S(2)}) %copy-start) | copy-done | bytes 311320
  2.3 0.0 copy-start.1
  2.3 0.8 %copy-done.1 = s32[2,8,512]{2,1,0:T(8,128)S(1)} copy-done((s32[2,8,512]{2,1,0:T(8,128)S(1)}, s32[2,8,512]{2,1,0:T(8,128)}, u32[]{:S(2)}) %copy-start.1) | copy-done | bytes 32792
  3.1 34.7 %two_steps.1 = (bf16[19,16,512]{2,1,0:T(8,128)(2,1)S(1)}, f32[2,128]{1,0:T(2,128)S(1)}) custom-call(s32[2,128]{1,0:T(2,128)S(1)} %bitcast.15, s32[2,128]{1,0:T(2,128)S(1)} %bitcast.16, f32[2,128]{1,0:T(2,128)S(1)} %bitcast.13, f32[2,128]{1,0:T(2,128)S(1)} %bitcast.14, s32[16,512]{1,0:T(8,128)S(1)} %bitcast.12, bf16[19,16,512]{2,1,0:T(8,128)(2,1)S(1)} %bitcast.11), custom_call_target="tpu_custom_call" | custom-call | tf_op jit(solution)/shard_map/two_steps/pallas_call | solution.py:424
  37.8 0.0 copy-start.6
  37.9 0.7 %copy-done.6 = f32[256]{0:T(256)S(1)} copy-done((f32[256]{0:T(256)S(1)}, f32[256]{0:T(256)}, u32[]{:S(2)}) %copy-start.6) | copy-done | bytes 1048
  38.5 0.6 %fusion.1 = (f32[256]{0:T(256)}, f32[256]{0:T(256)}) fusion(f32[256]{0:T(256)S(1)} %copy-done.6, f32[2,128]{1,0:T(2,128)S(1)} %get-tuple-element.6, f32[256]{0:T(256)S(1)} %copy-done.2, f32[256]{0:T(256)S(1)} %copy-done.3), kind=kLoop, calls=%fused_computation.2 | loop fusion | flops 1024 | bytes 6144 | tf_op jit(solution)/shard_map/sub | solution.py:454
  39.1 0.7 %copy.11 = bf16[19,2,8,512]{3,2,1,0:T(8,128)(2,1)} copy(bf16[19,2,8,512]{3,2,1,0:T(8,128)(2,1)S(1)} %bitcast.10) | data formatting | bytes 622592
Async XLA Ops:
  0.6 0.7 %copy-start.5 = (s32[256]{0:T(256)S(1)}, s32[256]{0:T(256)}, u32[]{:S(2)}) copy-start(s32[256]{0:T(256)} %param.13) | copy-start | bytes 3076
  0.6 0.7 %copy-start.3 = (f32[256]{0:T(256)S(1)}, f32[256]{0:T(256)}, u32[]{:S(2)}) copy-start(f32[256]{0:T(256)} %param.10) | copy-start | bytes 3076
  0.7 0.7 %copy-start.4 = (s32[256,1]{0,1:T(1,128)S(1)}, s32[256,1]{0,1:T(1,128)}, u32[]{:S(2)}) copy-start(s32[256,1]{0,1:T(1,128)} %param.12) | copy-start | bytes 3076
  0.7 0.7 %copy-start.2 = (f32[256]{0:T(256)S(1)}, f32[256]{0:T(256)}, u32[]{:S(2)}) copy-start(f32[256]{0:T(256)} %param.9) | copy-start | bytes 3076
  1.4 1.0 %copy-start = (bf16[19,2,8,512]{3,2,1,0:T(8,128)(2,1)S(1)}, bf16[19,2,8,512]{3,2,1,0:T(8,128)(2,1)}, u32[]{:S(2)}) copy-start(bf16[19,2,8,512]{3,2,1,0:T(8,128)(2,1)} %param.7) | copy-start | bytes 933892
  2.3 0.8 %copy-start.1 = (s32[2,8,512]{2,1,0:T(8,128)S(1)}, s32[2,8,512]{2,1,0:T(8,128)}, u32[]{:S(2)}) copy-start(s32[2,8,512]{2,1,0:T(8,128)} %param.8) | copy-start | bytes 98308
  37.8 0.7 %copy-start.6 = (f32[256]{0:T(256)S(1)}, f32[256]{0:T(256)}, u32[]{:S(2)}) copy-start(f32[256]{0:T(256)} %param.11) | copy-start | bytes 3076

commit v3 on v2

--- a/solution.py
+++ b/solution.py
@@ -215,7 +215,7 @@
     )
 
 
-def step_pair(own, vox, rad, rate, solid, pops, out, answer, *scratch):
+def step_pair(own, vox, rad, rate, ice, solid, pops, out, answer, coefs, ices, *scratch):
     (own_v, vox_v, rad_v, rate_v, solid_v, pops_v, ask, asked, tell, told, rel, below, above, edge, left, right) = scratch[:16]
     (src, near, spread, work, post, dens, loads, sends, recvs, zsend, zrecv, xsend, xrecv, nsend, nrecv) = scratch[16:]
     gz, col = lax.axis_index("gz"), lax.axis_index("col")
@@ -225,7 +225,7 @@
     fetch = [
         pltpu.make_async_copy(a, b, loads.at[i])
         for i, (a, b) in enumerate(
-            [(own, own_v), (vox, vox_v), (rad, rad_v), (rate, rate_v), (solid, solid_v), (pops, pops_v)]
+            [(own, own_v), (vox, vox_v), (rad, rad_v), (rate, rate_v), (ice, ices), (solid, solid_v), (pops, pops_v)]
         )
     ]
     for c in fetch:
@@ -242,6 +242,8 @@
         c.wait()
     table, named, rank, coef = request_table(own_v, vox_v, rad_v, rate_v, z, d)
     ask[...] = table
+    coefs[0:1, :] = coef[:, 0:128]
+    coefs[1:2, :] = coef[:, 128:256]
 
     def first(i, carry):
         lanes = pl.ds(pl.multiple_of(i * 128, 128), 128)
@@ -263,10 +265,10 @@
         remote(rel.at[pl.ds(0, 15)], below, zsend.at[0], zrecv.at[0], *up),
         remote(rel.at[pl.ds(5, 15)], above, zsend.at[1], zrecv.at[1], *down),
     ]
+    send_rows(ask, asked, sends.at[0], recvs.at[0], z, d, 1)
+    asked[0:1, :] = ask[0:1, :]
     for c in zcopies:
         c.start()
-    send_rows(ask, asked, sends.at[0], recvs.at[0], z, d, 1)
-    asked[0:1, :] = ask[0:1, :]
 
     for c in zcopies:
         c.wait_recv()
@@ -418,14 +420,17 @@
 
 def body(populations, solid, radius, rate, ice_mass, owner, voxel):
     vm = pl.BlockSpec(memory_space=pltpu.VMEM)
-    anywhere = pl.BlockSpec(memory_space=pl.ANY)
+    hbm = pl.BlockSpec(memory_space=pltpu.HBM)
     sem = pltpu.SemaphoreType.DMA
+    pair = jax.ShapeDtypeStruct((2, 128), f32)
     small = [pltpu.VMEM((2, 128), jnp.int32)] * 2 + [pltpu.VMEM((2, 128), f32)] * 2
-    state, answer = pl.pallas_call(
+    operands = [x.reshape(2, 128) for x in (owner, voxel, radius, rate, ice_mass)]
+    operands += [solid.reshape(16, 512), populations.reshape(19, 16, 512)]
+    state, answer, coef, ice = pl.pallas_call(
         step_pair,
-        out_shape=(jax.ShapeDtypeStruct((19, 16, 512), bf16), jax.ShapeDtypeStruct((2, 128), f32)),
-        in_specs=[anywhere] * 6,
-        out_specs=(vm, vm),
+        out_shape=(jax.ShapeDtypeStruct((19, 16, 512), bf16), pair, pair, pair),
+        in_specs=[hbm] * 7,
+        out_specs=(vm,) * 4,
         scratch_shapes=small
         + [pltpu.VMEM((16, 512), jnp.int32), pltpu.VMEM((19, 16, 512), bf16)]
         + [pltpu.VMEM((128, 128), f32)] * 4
@@ -437,21 +442,14 @@
         + [pltpu.VMEM((3, 4, 96, 128), f32)]
         + [pltpu.VMEM((20, 4, 40, 128), f32)] * 2
         + [pltpu.VMEM((16, 512), f32)]
-        + [sem((6,))]
+        + [sem((7,))]
         + [sem((2,))] * 6
         + [sem((8,))] * 2,
         name="two_steps",
         compiler_params=pltpu.CompilerParams(collective_id=0, has_side_effects=True, vmem_limit_bytes=48 * 2**20),
-    )(
-        owner.reshape(2, 128),
-        voxel.reshape(2, 128),
-        radius.reshape(2, 128),
-        rate.reshape(2, 128),
-        solid.reshape(16, 512),
-        populations.reshape(19, 16, 512),
-    )
-    flux = rate * radius * radius * answer.reshape(-1)
-    return (state.reshape(populations.shape), flux, ice_mass - flux)
+    )(*[pltpu.with_memory_space_constraint(x, pltpu.HBM) for x in operands])
+    flux = coef * answer
+    return (state.reshape(populations.shape), flux.reshape(-1), (ice - flux).reshape(-1))
 
 
 def solution(mesh):

time: 40.1 us -> 34.1 us (0.85)
  local copies, waits for them, and re-layouts: 3.81 us -> 0.72 us
  Pallas kernels: 34.7 us -> 32 us
    unnamed x15 -> x1, local copies, waits for them, and re-layouts: 3.81 us -> 0.72 us
    pallas_call x1, Pallas kernels: 34.7 us -> 32 us  [body(): pl.pallas_call(step_pair, out_shape=(jax.ShapeDtypeStruct((19, 16, 512),...]
    reshape x0 -> x1, other arithmetic: none -> 0.57 us  [body(): (ice - flux).reshape(-1)]
    sub x1 -> x0, other arithmetic: 0.57 us -> none  [body(): return (state.reshape(populations.shape), flux, ice_mass - flux)]
where the time goes in v3:
time: 34.1 us; the launch traced here: 34 us
  Pallas kernels  32 us (94%)
  local copies, waits for them, and re-layouts  0.72 us (2%)
  between operations  0.64 us (2%)
  other arithmetic  0.57 us (2%)
    pallas_call x1, Pallas kernels, body(): pl.pallas_call(step_pair, out_shape=(jax.ShapeDtypeStruct((19, 16, 512),...  32 us
    unnamed x1, local copies, waits for them, and re-layouts  0.72 us

profile of v3, /device:TPU:1, one launch (start us, length us, event | category | flops | bytes accessed | tf_op | source)
XLA Modules:
  0.0 34.0 jit_solution(14429761114754054813)
XLA Ops:
  0.6 32.0 %two_steps.1 = (bf16[19,16,512]{2,1,0:T(8,128)(2,1)S(1)}, f32[2,128]{1,0:T(2,128)S(1)}, f32[2,128]{1,0:T(2,128)S(1)}, f32[2,128]{1,0:T(2,128)S(1)}) custom-call(s32[2,128]{1,0:T(2,128)} %bitcast.15, s32[2,128]{1,0:T(2,128)} %bitcast.16, f32[2,128]{1,0:T(2,128)} %bitcast.17, f32[2,128]{1,0:T(2,128)} %bitcast.18, f32[2,128]{1,0:T(2,128)} %bitcast.19, ...), custom_call_target="tpu_custom_call" | custom-call | tf_op jit(solution)/shard_map/two_steps/pallas_call | solution.py:429
  32.7 0.6 %subtract_bitcast_fusion = (f32[256]{0:T(256)}, f32[256]{0:T(256)}) fusion(f32[2,128]{1,0:T(2,128)S(1)} %get-tuple-element.10, f32[2,128]{1,0:T(2,128)S(1)} %get-tuple-element.8, f32[2,128]{1,0:T(2,128)S(1)} %get-tuple-element.9), kind=kLoop, calls=%fused_computation | loop fusion | flops 512 | bytes 5120 | tf_op jit(solution)/shard_map/reshape | solution.py:452
  33.2 0.7 %copy.11 = bf16[19,2,8,512]{3,2,1,0:T(8,128)(2,1)} copy(bf16[19,2,8,512]{3,2,1,0:T(8,128)(2,1)S(1)} %bitcast.12) | data formatting | bytes 622592

commit v4 on v3

--- a/solution.py
+++ b/solution.py
@@ -18,6 +18,9 @@
 
 PEERS = sorted([(o, e) for o in range(8) for e in range(16) if (o, e) != (0, 0)], key=lambda p: -hops(p))
 
+FAR = [p for p in PEERS if hops(p) >= 4.5]
+CLOSE = [p for p in PEERS if hops(p) < 4.5]
+
 
 def peer(z, d, o, e):
     return lax.rem(z + o, 8) * 16 + lax.rem(d + e, 16)
@@ -28,8 +31,8 @@
         pl.semaphore_signal(sem, inc=1, device_id={"gz": peer(z, d, o, e)}, device_id_type=MESH)
 
 
-def send_rows(src, dst, send, recv, z, d, sign):
-    for o, e in PEERS:
+def send_rows(src, dst, send, recv, z, d, sign, peers):
+    for o, e in peers:
         row = pl.ds(o * 16 + e, 1)
         to = peer(z, d, o, e) if sign > 0 else peer(z, d, (8 - o) % 8, (16 - e) % 16)
         pltpu.make_async_remote_copy(
@@ -78,28 +81,42 @@
     return dot_t(named, value), named, rank, coef
 
 
-def serve(table, density):
+def parts(x):
+    high = x.astype(bf16)
+    rest = x - high.astype(f32)
+    middle = rest.astype(bf16)
+    return [high, middle, (rest - middle.astype(f32)).astype(bf16)]
+
+
+def lookup_field(density):
+    field = jnp.concatenate([density[:, c * 128 : (c + 1) * 128] for c in range(4)], axis=0)
+    return jnp.concatenate(parts(jnp.transpose(field)), axis=1)
+
+
+def look_up(table, field):
     rows = jnp.transpose(table)
     coef = jnp.concatenate([rows[k : k + 1, :] for k in range(4)], axis=1)
     code = jnp.concatenate([rows[k : k + 1, :] for k in range(4, 8)], axis=1).astype(jnp.int32)
     hi = ((code >> 7) & 3) * 16 + (code >> 9)
-    lo = code & 127
-    at_hi = (iota((128, 512), 0) == hi).astype(f32)
-    at_lo = iota((128, 512), 0) == lo
-    field = jnp.concatenate([density[:, c * 128 : (c + 1) * 128] for c in range(4)] + [jnp.zeros((64, 128), f32)], axis=0)
-    picked = dot(jnp.transpose(field), at_hi)
-    rho = jnp.sum(jnp.where(at_lo, picked, 0.0), axis=0, keepdims=True)
-    answer = 2.0 - rho
-    spread = jnp.where(at_lo, 0.5 * coef * answer, 0.0)
-    total = dot_t(at_hi, spread)
-    source = jnp.concatenate([total[c * 16 : (c + 1) * 16, :] for c in range(4)], axis=1)
-    reply = jnp.concatenate([answer[:, k * 128 : (k + 1) * 128] for k in range(4)] + [jnp.zeros((124, 128), f32)], axis=0)
-    return jnp.transpose(reply), source
+    at_lo = iota((128, 512), 0) == (code & 127)
+    at_hi = ((iota((192, 512), 0) & 63) == hi).astype(f32).astype(bf16)
+    picked = jnp.dot(field, at_hi, preferred_element_type=f32)
+    answer = 2.0 - jnp.sum(jnp.where(at_lo, picked, 0.0), axis=0, keepdims=True)
+    reply = jnp.concatenate([answer[:, k * 128 : (k + 1) * 128] for k in range(4)] + [jnp.zeros((4, 128), f32)], axis=0)
+    return jnp.transpose(reply), (coef * answer, at_lo, at_hi[0:64])
+
+
+def scatter(flux, at_lo, at_hi):
+    spread = jnp.concatenate(parts(jnp.where(at_lo, 0.5 * flux, 0.0)), axis=1)
+    where = jnp.concatenate([at_hi] * 3, axis=1)
+    total = lax.dot_general(where, spread, (((1,), (1,)), ((), ())), preferred_element_type=f32)
+    return jnp.concatenate([total[c * 16 : (c + 1) * 16, :] for c in range(4)], axis=1)
 
 
 def read_reply(reply, named, rank):
-    rows = jnp.transpose(reply)[0:8, :]
-    got = dot(rows, named)
+    rows = jnp.transpose(reply)
+    got = jnp.dot(jnp.concatenate(parts(rows), axis=0), named, preferred_element_type=f32)
+    got = got[0:8] + got[8:16] + got[16:24]
     return jnp.sum(jnp.where(iota((8, 256), 0) == rank, got, 0.0), axis=0, keepdims=True)
 
 
@@ -215,9 +232,9 @@
     )
 
 
-def step_pair(own, vox, rad, rate, ice, solid, pops, out, answer, coefs, ices, *scratch):
-    (own_v, vox_v, rad_v, rate_v, solid_v, pops_v, ask, asked, tell, told, rel, below, above, edge, left, right) = scratch[:16]
-    (src, near, spread, work, post, dens, loads, sends, recvs, zsend, zrecv, xsend, xrecv, nsend, nrecv) = scratch[16:]
+def step_pair(own, vox, rad, rate, ice, solid, pops, out, flux, ice_left, *scratch):
+    (own_v, vox_v, rad_v, rate_v, ice_v, solid_v, pops_v, ask, asked, tell, told, rel, below, above, edge, left, right) = scratch[:17]
+    (src, near, spread, work, post, dens, field, named_ref, loads, sends, recvs, zsend, zrecv, xsend, xrecv, nsend, nrecv) = scratch[17:]
     gz, col = lax.axis_index("gz"), lax.axis_index("col")
     z, d = gz // 16, lax.rem(gz, 16)
     barrier = pltpu.get_barrier_semaphore()
@@ -225,7 +242,7 @@
     fetch = [
         pltpu.make_async_copy(a, b, loads.at[i])
         for i, (a, b) in enumerate(
-            [(own, own_v), (vox, vox_v), (rad, rad_v), (rate, rate_v), (ice, ices), (solid, solid_v), (pops, pops_v)]
+            [(own, own_v), (vox, vox_v), (rad, rad_v), (rate, rate_v), (ice, ice_v), (solid, solid_v), (pops, pops_v)]
         )
     ]
     for c in fetch:
@@ -242,8 +259,7 @@
         c.wait()
     table, named, rank, coef = request_table(own_v, vox_v, rad_v, rate_v, z, d)
     ask[...] = table
-    coefs[0:1, :] = coef[:, 0:128]
-    coefs[1:2, :] = coef[:, 128:256]
+    named_ref[...] = named.astype(bf16)
 
     def first(i, carry):
         lanes = pl.ds(pl.multiple_of(i * 128, 128), 128)
@@ -255,6 +271,7 @@
         return carry
 
     lax.fori_loop(0, 4, first, 0)
+    field[...] = lookup_field(dens[...])
     for q in range(19):
         rel[ZPLACE[q]] = lane_roll(wide(post, q, pl.ds(0, 16)), VELOCITIES[q][2]).astype(bf16)
     rel[ZPLACE[FLAG]] = jnp.where(solid_v[...] > 0, 1.0, 0.0).astype(bf16)
@@ -265,7 +282,7 @@
         remote(rel.at[pl.ds(0, 15)], below, zsend.at[0], zrecv.at[0], *up),
         remote(rel.at[pl.ds(5, 15)], above, zsend.at[1], zrecv.at[1], *down),
     ]
-    send_rows(ask, asked, sends.at[0], recvs.at[0], z, d, 1)
+    send_rows(ask, asked, sends.at[0], recvs.at[0], z, d, 1, PEERS)
     asked[0:1, :] = ask[0:1, :]
     for c in zcopies:
         c.start()
@@ -307,15 +324,17 @@
         c.start()
 
     wait_rows(asked, recvs.at[0])
-    reply, total = serve(asked[...], dens[...])
+    reply, slots = look_up(asked[:, 0:8], field[...])
+    tell[:, 0:8] = reply
+    send_rows(tell, told, sends.at[1], recvs.at[1], z, d, -1, FAR)
+    total = scatter(*slots)
     src[...] = jnp.where(solid_v[...] > 0, 0.0, total).astype(bf16)
     ncopies = []
     for i, (dz, dx) in enumerate(NEAR):
         ncopies.append(remote(src, near.at[7 - i], nsend.at[i], nrecv.at[7 - i], *beside(dz, dx)))
     for c in ncopies:
         c.start()
-    tell[...] = reply
-    send_rows(tell, told, sends.at[1], recvs.at[1], z, d, -1)
+    send_rows(tell, told, sends.at[1], recvs.at[1], z, d, -1, CLOSE)
     told[0:1, :] = tell[0:1, :]
 
     for c in xcopies:
@@ -409,13 +428,23 @@
         out[q] = lane_roll(moved, cy).astype(bf16)
 
     wait_rows(told, recvs.at[1])
-    line = read_reply(told[...], named, rank)
-    answer[0:1, :] = line[:, 0:128]
-    answer[1:2, :] = line[:, 128:256]
+    line = coef * read_reply(told[:, 0:8], named_ref[...], rank)
+    for k in (0, 1):
+        row = line[:, 128 * k : 128 * k + 128]
+        flux[k : k + 1, :] = row
+        ice_left[k : k + 1, :] = ice_v[k : k + 1, :] - row
     wait_rows(ask, sends.at[0])
     wait_rows(tell, sends.at[1])
     for c in zcopies + xcopies + ncopies:
         c.wait_send()
+
+
+def hand_over(a, b, c, x, y, z, sems):
+    copies = [pltpu.make_async_copy(s, t, sems.at[i]) for i, (s, t) in enumerate([(a, x), (b, y), (c, z)])]
+    for one in copies:
+        one.start()
+    for one in copies:
+        one.wait()
 
 
 def body(populations, solid, radius, rate, ice_mass, owner, voxel):
@@ -423,14 +452,14 @@
     hbm = pl.BlockSpec(memory_space=pltpu.HBM)
     sem = pltpu.SemaphoreType.DMA
     pair = jax.ShapeDtypeStruct((2, 128), f32)
-    small = [pltpu.VMEM((2, 128), jnp.int32)] * 2 + [pltpu.VMEM((2, 128), f32)] * 2
+    small = [pltpu.VMEM((2, 128), jnp.int32)] * 2 + [pltpu.VMEM((2, 128), f32)] * 3
     operands = [x.reshape(2, 128) for x in (owner, voxel, radius, rate, ice_mass)]
     operands += [solid.reshape(16, 512), populations.reshape(19, 16, 512)]
-    state, answer, coef, ice = pl.pallas_call(
+    moved = pl.pallas_call(
         step_pair,
-        out_shape=(jax.ShapeDtypeStruct((19, 16, 512), bf16), pair, pair, pair),
+        out_shape=(jax.ShapeDtypeStruct((19, 16, 512), bf16), pair, pair),
         in_specs=[hbm] * 7,
-        out_specs=(vm,) * 4,
+        out_specs=(vm,) * 3,
         scratch_shapes=small
         + [pltpu.VMEM((16, 512), jnp.int32), pltpu.VMEM((19, 16, 512), bf16)]
         + [pltpu.VMEM((128, 128), f32)] * 4
@@ -441,15 +470,23 @@
         + [pltpu.VMEM((16, 512), bf16), pltpu.VMEM((8, 16, 512), bf16)]
         + [pltpu.VMEM((3, 4, 96, 128), f32)]
         + [pltpu.VMEM((20, 4, 40, 128), f32)] * 2
-        + [pltpu.VMEM((16, 512), f32)]
+        + [pltpu.VMEM((16, 512), f32), pltpu.VMEM((128, 192), bf16), pltpu.VMEM((128, 256), bf16)]
         + [sem((7,))]
         + [sem((2,))] * 6
         + [sem((8,))] * 2,
         name="two_steps",
         compiler_params=pltpu.CompilerParams(collective_id=0, has_side_effects=True, vmem_limit_bytes=48 * 2**20),
     )(*[pltpu.with_memory_space_constraint(x, pltpu.HBM) for x in operands])
-    flux = coef * answer
-    return (state.reshape(populations.shape), flux.reshape(-1), (ice - flux).reshape(-1))
+    state, flux, ice_left = pl.pallas_call(
+        hand_over,
+        out_shape=(jax.ShapeDtypeStruct((19, 16, 512), bf16), pair, pair),
+        in_specs=[vm] * 3,
+        out_specs=(hbm,) * 3,
+        scratch_shapes=[sem((3,))],
+        name="hand_over",
+        compiler_params=pltpu.CompilerParams(vmem_limit_bytes=4 * 2**20),
+    )(*[pltpu.with_memory_space_constraint(x, pltpu.VMEM) for x in moved])
+    return (state.reshape(populations.shape), flux.reshape(-1), ice_left.reshape(-1))
 
 
 def solution(mesh):

time: 34.1 us -> 33 us (0.968)
  local copies, waits for them, and re-layouts: 0.72 us -> 0 us
  other arithmetic: 0.57 us -> 0 us
    pallas_call x0 -> x1, Pallas kernels: none -> 0.75 us  [body(): pl.pallas_call(hand_over, out_shape=(jax.ShapeDtypeStruct((19, 16, 512),...]
    unnamed x1 -> x0, local copies, waits for them, and re-layouts: 0.72 us -> none
    reshape x1 -> x0, other arithmetic: 0.57 us -> none  [body(): (ice - flux).reshape(-1)]
    pallas_call x1, Pallas kernels: 32 us -> 31.5 us  [body(): pl.pallas_call(step_pair, out_shape=(jax.ShapeDtypeStruct((19, 16, 512),...]
where the time goes in v4:
time: 33 us; the launch traced here: 32.9 us
  Pallas kernels  32.2 us (98%)
  between operations  0.64 us (2%)
    pallas_call x1, Pallas kernels, body(): pl.pallas_call(step_pair, out_shape=(jax.ShapeDtypeStruct((19, 16, 512),...  31.5 us
    pallas_call x1, Pallas kernels, body(): pl.pallas_call(hand_over, out_shape=(jax.ShapeDtypeStruct((19, 16, 512),...  0.75 us

profile of v4, /device:TPU:1, one launch (start us, length us, event | category | flops | bytes accessed | tf_op | source)
XLA Modules:
  0.0 32.9 jit_solution(6166746107799778849)
XLA Ops:
  0.6 31.5 %two_steps.1 = (bf16[19,16,512]{2,1,0:T(8,128)(2,1)S(1)}, f32[2,128]{1,0:T(2,128)S(1)}, f32[2,128]{1,0:T(2,128)S(1)}) custom-call(s32[2,128]{1,0:T(2,128)} %bitcast.12, s32[2,128]{1,0:T(2,128)} %bitcast.13, f32[2,128]{1,0:T(2,128)} %bitcast.14, f32[2,128]{1,0:T(2,128)} %bitcast.15, f32[2,128]{1,0:T(2,128)} %bitcast.16, s32[16,512]{1,0:T(8,128)} %bitcast.11, ...), custom_call_target="tpu_custom_call" | custom-call | tf_op jit(solution)/shard_map/two_steps/pallas_call | solution.py:458
  32.1 0.8 %hand_over.1 = (bf16[19,16,512]{2,1,0:T(8,128)(2,1)}, f32[2,128]{1,0:T(2,128)}, f32[2,128]{1,0:T(2,128)}) custom-call(bf16[19,16,512]{2,1,0:T(8,128)(2,1)S(1)} %get-tuple-element.9.a, f32[2,128]{1,0:T(2,128)S(1)} %get-tuple-element.10.b, f32[2,128]{1,0:T(2,128)S(1)} %get-tuple-element.11.c), custom_call_target="tpu_custom_call" | custom-call | tf_op jit(solution)/shard_map/hand_over/pallas_call | solution.py:480

commit v5 on v4

--- a/solution.py
+++ b/solution.py
@@ -18,8 +18,7 @@
 
 PEERS = sorted([(o, e) for o in range(8) for e in range(16) if (o, e) != (0, 0)], key=lambda p: -hops(p))
 
-FAR = [p for p in PEERS if hops(p) >= 4.5]
-CLOSE = [p for p in PEERS if hops(p) < 4.5]
+TURNS = sorted(range(16), key=lambda e: -min(e, 16 - e))
 
 
 def peer(z, d, o, e):
@@ -31,23 +30,46 @@
         pl.semaphore_signal(sem, inc=1, device_id={"gz": peer(z, d, o, e)}, device_id_type=MESH)
 
 
-def send_rows(src, dst, send, recv, z, d, sign, peers):
-    for o, e in peers:
-        row = pl.ds(o * 16 + e, 1)
-        to = peer(z, d, o, e) if sign > 0 else peer(z, d, (8 - o) % 8, (16 - e) % 16)
-        pltpu.make_async_remote_copy(
-            src_ref=src.at[row],
-            dst_ref=dst.at[row],
-            send_sem=send,
-            recv_sem=recv,
-            device_id={"gz": to},
-            device_id_type=MESH,
-        ).start()
-
-
-def wait_rows(buf, sem):
-    rows = buf.at[pl.ds(1, 127)]
+def rows_of(place):
+    return pl.ds(pl.multiple_of(2 * place, 2), 2)
+
+
+def rows_copy(src, dst, send, recv, gz):
+    return pltpu.make_async_remote_copy(
+        src_ref=src, dst_ref=dst, send_sem=send, recv_sem=recv, device_id={"gz": gz}, device_id_type=MESH
+    )
+
+
+def wait_bytes(rows, sem):
     pltpu.make_async_copy(rows, rows, sem).wait()
+
+
+def send_requests(ask, asked, send, recv, z, d):
+    half, level = z // 4, lax.rem(z, 4)
+    for e in TURNS:
+        for there in range(4):
+            src = ask.at[rows_of(there * 16 + e)]
+            dst = asked.at[half, rows_of(level * 16 + e)]
+            copy = rows_copy(src, dst, send, recv.at[half], there * 16 + lax.rem(d + e, 16))
+            if e:
+                copy.start()
+            else:
+                pl.when(z != there)(copy.start)
+                pl.when(z == there)(pltpu.make_async_copy(src, dst, recv.at[half]).start)
+
+
+def send_answers(tell, told, send, recv, half, z, d):
+    for e in TURNS:
+        for level in range(4):
+            src = tell.at[half, rows_of(level * 16 + e)]
+            dst = told.at[rows_of(z * 16 + e)]
+            to = 4 * half + level
+            copy = rows_copy(src, dst, send, recv, to * 16 + lax.rem(d + 16 - e, 16))
+            if e or half:
+                copy.start()
+            else:
+                pl.when(z != to)(copy.start)
+                pl.when(z == to)(pltpu.make_async_copy(src, dst, recv).start)
 
 
 def iota(shape, dim):
@@ -66,11 +88,12 @@
     return jnp.dot(a, b, precision=HIGHEST, preferred_element_type=f32)
 
 
-def request_table(own_ref, vox_ref, rad_ref, rate_ref, z, d):
+def request_table(own_ref, vox_ref, rad_ref, rate_ref, d):
     own, vox = flat_row(own_ref), flat_row(vox_ref)
     rad, rate = flat_row(rad_ref), flat_row(rate_ref)
     coef = rate * rad * rad
-    rel = (((own >> 4) - z) & 7) * 16 + (((own & 15) - d) & 15)
+    level, upper = own >> 4, own >> 6
+    rel = 2 * (jnp.where(upper > 0, 7 - level, level) * 16 + (((own & 15) - d) & 15)) + upper
     named = (iota((128, 256), 0) == rel).astype(f32)
     earlier = (iota((256, 256), 0) < iota((256, 256), 1)).astype(bf16)
     before = jnp.dot(named.astype(bf16), earlier, preferred_element_type=f32)
@@ -88,8 +111,8 @@
     return [high, middle, (rest - middle.astype(f32)).astype(bf16)]
 
 
-def lookup_field(density):
-    field = jnp.concatenate([density[:, c * 128 : (c + 1) * 128] for c in range(4)], axis=0)
+def lookup_field(own, other):
+    field = jnp.concatenate([x[:, c * 128 : (c + 1) * 128] for x in (own, other) for c in range(4)], axis=0)
     return jnp.concatenate(parts(jnp.transpose(field)), axis=1)
 
 
@@ -97,20 +120,23 @@
     rows = jnp.transpose(table)
     coef = jnp.concatenate([rows[k : k + 1, :] for k in range(4)], axis=1)
     code = jnp.concatenate([rows[k : k + 1, :] for k in range(4, 8)], axis=1).astype(jnp.int32)
-    hi = ((code >> 7) & 3) * 16 + (code >> 9)
+    hi = (iota((1, 512), 1) & 1) * 64 + ((code >> 7) & 3) * 16 + (code >> 9)
     at_lo = iota((128, 512), 0) == (code & 127)
-    at_hi = ((iota((192, 512), 0) & 63) == hi).astype(f32).astype(bf16)
+    at_hi = ((iota((384, 512), 0) & 127) == hi).astype(f32).astype(bf16)
     picked = jnp.dot(field, at_hi, preferred_element_type=f32)
     answer = 2.0 - jnp.sum(jnp.where(at_lo, picked, 0.0), axis=0, keepdims=True)
     reply = jnp.concatenate([answer[:, k * 128 : (k + 1) * 128] for k in range(4)] + [jnp.zeros((4, 128), f32)], axis=0)
-    return jnp.transpose(reply), (coef * answer, at_lo, at_hi[0:64])
+    return jnp.transpose(reply), (coef * answer, at_lo, at_hi[0:128])
 
 
 def scatter(flux, at_lo, at_hi):
     spread = jnp.concatenate(parts(jnp.where(at_lo, 0.5 * flux, 0.0)), axis=1)
     where = jnp.concatenate([at_hi] * 3, axis=1)
-    total = lax.dot_general(where, spread, (((1,), (1,)), ((), ())), preferred_element_type=f32)
-    return jnp.concatenate([total[c * 16 : (c + 1) * 16, :] for c in range(4)], axis=1)
+    return lax.dot_general(where, spread, (((1,), (1,)), ((), ())), preferred_element_type=f32)
+
+
+def block_of(total, k):
+    return jnp.concatenate([total[64 * k + 16 * c : 64 * k + 16 * c + 16, :] for c in range(4)], axis=1)
 
 
 def read_reply(reply, named, rank):
@@ -206,7 +232,7 @@
             out[q] = jnp.where(solid, g[q + 1], even + odd - 0.6 * g[q])
         if q + 1 in wanted:
             out[q + 1] = jnp.where(solid, g[q], even - odd - 0.6 * g[q + 1])
-    return out, rho
+    return out
 
 
 def wide(ref, q, rows):
@@ -233,8 +259,9 @@
 
 
 def step_pair(own, vox, rad, rate, ice, solid, pops, out, flux, ice_left, *scratch):
-    (own_v, vox_v, rad_v, rate_v, ice_v, solid_v, pops_v, ask, asked, tell, told, rel, below, above, edge, left, right) = scratch[:17]
-    (src, near, spread, work, post, dens, field, named_ref, loads, sends, recvs, zsend, zrecv, xsend, xrecv, nsend, nrecv) = scratch[17:]
+    (own_v, vox_v, rad_v, rate_v, ice_v, solid_v, pops_v, ask, asked, told, tell, rel, below, above, edge, left, right) = scratch[:17]
+    (src, near, spread, work, post, dens, named_ref, mdens, total, msrc, gsrc) = scratch[17:28]
+    (loads, ask_send, ask_recv, tell_send, tell_recv, pair_send, pair_recv, zsend, zrecv, xsend, xrecv, nsend, nrecv) = scratch[28:]
     gz, col = lax.axis_index("gz"), lax.axis_index("col")
     z, d = gz // 16, lax.rem(gz, 16)
     barrier = pltpu.get_barrier_semaphore()
@@ -247,48 +274,87 @@
     ]
     for c in fetch:
         c.start()
-    greet_group(barrier, z, d)
+    server, partner = z < 4, (7 - z) * 16 + d
 
     def beside(dz, dx):
         return lax.rem(gz + dz + 128, 128), lax.rem(col + dx + 4, 4)
 
-    for dz, dx in ASIDE:
+    for dz, dx in NEAR:
         g, c = beside(dz, dx)
         pl.semaphore_signal(barrier, inc=1, device_id={"gz": g, "col": c}, device_id_type=MESH)
-    for c in fetch:
+
+    @pl.when(server)
+    def _():
+        greet_group(barrier, z, d)
+
+    for c in fetch[:5]:
         c.wait()
-    table, named, rank, coef = request_table(own_v, vox_v, rad_v, rate_v, z, d)
+    table, named, rank, coef = request_table(own_v, vox_v, rad_v, rate_v, d)
     ask[...] = table
     named_ref[...] = named.astype(bf16)
+    for c in fetch[5:]:
+        c.wait()
+    for k in range(4):
+        lanes = pl.ds(128 * k, 128)
+        dens[:, lanes] = density_of([pops_v[q, :, lanes].astype(f32) for q in range(19)])
 
     def first(i, carry):
         lanes = pl.ds(pl.multiple_of(i * 128, 128), 128)
         g = [pops_v[q, :, lanes].astype(f32) for q in range(19)]
-        made, rho = collide(g, solid_v[:, lanes] > 0, None, range(19))
-        dens[:, lanes] = rho
+        made = collide(g, solid_v[:, lanes] > 0, None, range(19))
         for q in range(19):
             post[q, i, 0:16, :] = made[q]
         return carry
 
-    lax.fori_loop(0, 4, first, 0)
-    field[...] = lookup_field(dens[...])
-    for q in range(19):
-        rel[ZPLACE[q]] = lane_roll(wide(post, q, pl.ds(0, 16)), VELOCITIES[q][2]).astype(bf16)
-    rel[ZPLACE[FLAG]] = jnp.where(solid_v[...] > 0, 1.0, 0.0).astype(bf16)
-
-    pl.semaphore_wait(barrier, 127 + len(ASIDE))
-    up, down = beside(1, 0), beside(-1, 0)
+    def collide_first():
+        lax.fori_loop(0, 4, first, 0)
+        for q in range(19):
+            rel[ZPLACE[q]] = lane_roll(wide(post, q, pl.ds(0, 16)), VELOCITIES[q][2]).astype(bf16)
+        rel[ZPLACE[FLAG]] = jnp.where(solid_v[...] > 0, 1.0, 0.0).astype(bf16)
+
+    @pl.when(server)
+    def _():
+        collide_first()
+
+    pl.semaphore_wait(barrier, len(NEAR) + jnp.where(server, 63, 64))
+    density_copy = rows_copy(dens, mdens, pair_send.at[0], pair_recv.at[0], partner)
+    source_copy = rows_copy(msrc, gsrc, pair_send.at[1], pair_recv.at[1], partner)
+
+    pl.when(jnp.logical_not(server))(density_copy.start)
+    send_requests(ask, asked, ask_send, ask_recv, z, d)
+    pl.when(jnp.logical_not(server))(collide_first)
+
+    def within(dz):
+        return {-1: gz > 0, 0: None, 1: gz < 127}[dz]
+
+    def if_within(dz, act):
+        if dz:
+            pl.when(within(dz))(act)
+        else:
+            act()
+
     zcopies = [
-        remote(rel.at[pl.ds(0, 15)], below, zsend.at[0], zrecv.at[0], *up),
-        remote(rel.at[pl.ds(5, 15)], above, zsend.at[1], zrecv.at[1], *down),
+        remote(rel.at[pl.ds(0, 15)], below, zsend.at[0], zrecv.at[0], *beside(1, 0)),
+        remote(rel.at[pl.ds(5, 15)], above, zsend.at[1], zrecv.at[1], *beside(-1, 0)),
     ]
-    send_rows(ask, asked, sends.at[0], recvs.at[0], z, d, 1, PEERS)
-    asked[0:1, :] = ask[0:1, :]
-    for c in zcopies:
-        c.start()
-
-    for c in zcopies:
-        c.wait_recv()
+    if_within(1, zcopies[0].start)
+    if_within(-1, zcopies[1].start)
+
+    def answer_half(half):
+        wait_bytes(asked.at[half], ask_recv.at[half])
+        reply, slots = look_up(asked[half, :, 0:8], lookup_field(dens[...], mdens[...]))
+        tell[half, :, 0:8] = reply
+        return slots
+
+    @pl.when(server)
+    def _():
+        density_copy.wait_recv()
+        slots = answer_half(0)
+        send_answers(tell, told, tell_send, tell_recv, 0, z, d)
+        total[...] = scatter(*slots)
+
+    if_within(-1, zcopies[0].wait_recv)
+    if_within(1, zcopies[1].wait_recv)
     has_below, has_above = gz > 0, gz < 127
     for q in range(20):
         cz, i = VELOCITIES[q][0], ZPLACE[q]
@@ -323,19 +389,26 @@
     for c in xcopies:
         c.start()
 
-    wait_rows(asked, recvs.at[0])
-    reply, slots = look_up(asked[:, 0:8], field[...])
-    tell[:, 0:8] = reply
-    send_rows(tell, told, sends.at[1], recvs.at[1], z, d, -1, FAR)
-    total = scatter(*slots)
-    src[...] = jnp.where(solid_v[...] > 0, 0.0, total).astype(bf16)
+    @pl.when(server)
+    def _():
+        both = total[...] + scatter(*answer_half(1))
+        msrc[...] = block_of(both, 1).astype(bf16)
+        source_copy.start()
+        src[...] = jnp.where(solid_v[...] > 0, 0.0, block_of(both, 0)).astype(bf16)
+
+    @pl.when(jnp.logical_not(server))
+    def _():
+        source_copy.wait_recv()
+        src[...] = jnp.where(solid_v[...] > 0, 0.0, gsrc[...].astype(f32)).astype(bf16)
+
     ncopies = []
     for i, (dz, dx) in enumerate(NEAR):
         ncopies.append(remote(src, near.at[7 - i], nsend.at[i], nrecv.at[7 - i], *beside(dz, dx)))
-    for c in ncopies:
-        c.start()
-    send_rows(tell, told, sends.at[1], recvs.at[1], z, d, -1, CLOSE)
-    told[0:1, :] = tell[0:1, :]
+        if_within(dz, ncopies[-1].start)
+
+    @pl.when(server)
+    def _():
+        send_answers(tell, told, tell_send, tell_recv, 1, z, d)
 
     for c in xcopies:
         c.wait_recv()
@@ -360,8 +433,8 @@
             put(work, q, pl.ds(0, 32), row_roll(wide(work, q, pl.ds(0, 32)), cx))
             put(work, q, pl.ds(0 if cx == 1 else 7, 4, stride=8), ends[0:4])
 
-    for i in range(8):
-        remote(src, near.at[i], nsend.at[7 - i], nrecv.at[i], gz, col).wait_recv()
+    for i, (dz, dx) in enumerate(NEAR):
+        if_within(dz, ncopies[7 - i].wait_recv)
     for a in (-1, 0, 1):
         for b in (-1, 0, 1):
             there = True
@@ -409,7 +482,7 @@
         for r, wanted, inside in jobs:
             rows = pl.ds(r, 8)
             g = [work[q, i, rows, :] for q in range(19)]
-            made, _ = collide(g, work[FLAG, i, rows, :] > 0.5, post[FLAG, i, rows, :], wanted)
+            made = collide(g, work[FLAG, i, rows, :] > 0.5, post[FLAG, i, rows, :], wanted)
             for q in wanted:
                 post[q, i, rows, :] = made[q] if inside is None else jnp.where(inside, made[q], 0.0)
         return carry
@@ -427,16 +500,30 @@
                 moved = jnp.where(iota((16, 512), 0) == at, wide(post, q, pl.ds(rim + k, 1)), moved)
         out[q] = lane_roll(moved, cy).astype(bf16)
 
-    wait_rows(told, recvs.at[1])
+    wait_bytes(told, tell_recv)
     line = coef * read_reply(told[:, 0:8], named_ref[...], rank)
     for k in (0, 1):
         row = line[:, 128 * k : 128 * k + 128]
         flux[k : k + 1, :] = row
         ice_left[k : k + 1, :] = ice_v[k : k + 1, :] - row
-    wait_rows(ask, sends.at[0])
-    wait_rows(tell, sends.at[1])
-    for c in zcopies + xcopies + ncopies:
+    if_within(1, zcopies[0].wait_send)
+    if_within(-1, zcopies[1].wait_send)
+    for c in xcopies:
         c.wait_send()
+    for i, (dz, dx) in enumerate(NEAR):
+        if_within(dz, ncopies[i].wait_send)
+
+    @pl.when(server)
+    def _():
+        wait_bytes(ask.at[pl.ds(0, 126)], ask_send)
+        wait_bytes(tell.at[0, pl.ds(0, 126)], tell_send)
+        wait_bytes(tell.at[1], tell_send)
+        source_copy.wait_send()
+
+    @pl.when(jnp.logical_not(server))
+    def _():
+        wait_bytes(ask, ask_send)
+        density_copy.wait_send()
 
 
 def hand_over(a, b, c, x, y, z, sems):
@@ -462,7 +549,7 @@
         out_specs=(vm,) * 3,
         scratch_shapes=small
         + [pltpu.VMEM((16, 512), jnp.int32), pltpu.VMEM((19, 16, 512), bf16)]
-        + [pltpu.VMEM((128, 128), f32)] * 4
+        + [pltpu.VMEM((128, 128), f32), pltpu.VMEM((2, 128, 128), f32)] * 2
         + [pltpu.VMEM((20, 16, 512), bf16)]
         + [pltpu.VMEM((15, 16, 512), bf16)] * 2
         + [pltpu.VMEM((11, 16, 512), bf16)]
@@ -470,8 +557,9 @@
         + [pltpu.VMEM((16, 512), bf16), pltpu.VMEM((8, 16, 512), bf16)]
         + [pltpu.VMEM((3, 4, 96, 128), f32)]
         + [pltpu.VMEM((20, 4, 40, 128), f32)] * 2
-        + [pltpu.VMEM((16, 512), f32), pltpu.VMEM((128, 192), bf16), pltpu.VMEM((128, 256), bf16)]
-        + [sem((7,))]
+        + [pltpu.VMEM((16, 512), f32), pltpu.VMEM((128, 256), bf16), pltpu.VMEM((16, 512), f32), pltpu.VMEM((128, 128), f32)]
+        + [pltpu.VMEM((16, 512), bf16)] * 2
+        + [sem((7,)), sem, sem((2,)), sem, sem]
         + [sem((2,))] * 6
         + [sem((8,))] * 2,
         name="two_steps",

time: 33 us -> 31.8 us (0.964)
  Pallas kernels: 32.2 us -> 31.1 us
    pallas_call x1, Pallas kernels: 31.5 us -> 30.3 us  [body(): pl.pallas_call(step_pair, out_shape=(jax.ShapeDtypeStruct((19, 16, 512),...]
where the time goes in v5:
time: 31.8 us; the launch traced here: 31.7 us
  Pallas kernels  31.1 us (98%)
  between operations  0.64 us (2%)
    pallas_call x1, Pallas kernels, body(): pl.pallas_call(step_pair, out_shape=(jax.ShapeDtypeStruct((19, 16, 512),...  30.3 us
    pallas_call x1, Pallas kernels, body(): pl.pallas_call(hand_over, out_shape=(jax.ShapeDtypeStruct((19, 16, 512),...  0.75 us

profile of v5, /device:TPU:1, one launch (start us, length us, event | category | flops | bytes accessed | tf_op | source)
XLA Modules:
  0.0 31.7 jit_solution(7658248418469007136)
XLA Ops:
  0.6 30.3 %two_steps.1 = (bf16[19,16,512]{2,1,0:T(8,128)(2,1)S(1)}, f32[2,128]{1,0:T(2,128)S(1)}, f32[2,128]{1,0:T(2,128)S(1)}) custom-call(s32[2,128]{1,0:T(2,128)} %bitcast.12, s32[2,128]{1,0:T(2,128)} %bitcast.13, f32[2,128]{1,0:T(2,128)} %bitcast.14, f32[2,128]{1,0:T(2,128)} %bitcast.15, f32[2,128]{1,0:T(2,128)} %bitcast.16, s32[16,512]{1,0:T(8,128)} %bitcast.11, ...), custom_call_target="tpu_custom_call" | custom-call | tf_op jit(solution)/shard_map/two_steps/pallas_call | solution.py:545
  31.0 0.8 %hand_over.1 = (bf16[19,16,512]{2,1,0:T(8,128)(2,1)}, f32[2,128]{1,0:T(2,128)}, f32[2,128]{1,0:T(2,128)}) custom-call(bf16[19,16,512]{2,1,0:T(8,128)(2,1)S(1)} %get-tuple-element.9.a, f32[2,128]{1,0:T(2,128)S(1)} %get-tuple-element.10.b, f32[2,128]{1,0:T(2,128)S(1)} %get-tuple-element.11.c), custom_call_target="tpu_custom_call" | custom-call | tf_op jit(solution)/shard_map/hand_over/pallas_call | solution.py:568

commit v6 on v5

--- a/solution.py
+++ b/solution.py
@@ -172,12 +172,9 @@
 UP = [q for q in range(19) if VELOCITIES[q][0] == 1]
 FLAT = [q for q in range(20) if VELOCITIES[q][0] == 0]
 DOWN = [q for q in range(19) if VELOCITIES[q][0] == -1]
-ZPLACE = {q: i for i, q in enumerate(UP + FLAT + DOWN)}
 XUP = [q for q in range(19) if VELOCITIES[q][1] == 1]
 XFLAT = [q for q in range(20) if VELOCITIES[q][1] == 0]
 XDOWN = [q for q in range(19) if VELOCITIES[q][1] == -1]
-XTILES = XUP + XUP[-1:] + XFLAT + XDOWN + XDOWN[-1:]
-XPLACE = {q: XTILES.index(q) for q in range(20)}
 NEAR = [(a, b) for a in (-1, 0, 1) for b in (-1, 0, 1) if (a, b) != (0, 0)]
 ASIDE = [(a, b) for a, b in NEAR if b != 0]
 
@@ -309,8 +306,18 @@
     def collide_first():
         lax.fori_loop(0, 4, first, 0)
         for q in range(19):
-            rel[ZPLACE[q]] = lane_roll(wide(post, q, pl.ds(0, 16)), VELOCITIES[q][2]).astype(bf16)
-        rel[ZPLACE[FLAG]] = jnp.where(solid_v[...] > 0, 1.0, 0.0).astype(bf16)
+            if VELOCITIES[q][0]:
+                at = UP.index(q) if q in UP else 15 + DOWN.index(q)
+                rel[at] = lane_roll(wide(post, q, pl.ds(0, 16)), VELOCITIES[q][2]).astype(bf16)
+        for k in range(5):
+            two = []
+            for q in FLAT[2 * k : 2 * k + 2]:
+                if q == FLAG:
+                    two.append(jnp.where(solid_v[...] > 0, 1.0, 0.0))
+                else:
+                    two.append(lane_roll(wide(post, q, pl.ds(0, 16)), VELOCITIES[q][2]))
+            rel[5 + k] = jnp.concatenate([x[8:16] for x in two], axis=0).astype(bf16)
+            rel[10 + k] = jnp.concatenate([x[0:8] for x in two], axis=0).astype(bf16)
 
     @pl.when(server)
     def _():
@@ -334,8 +341,8 @@
             act()
 
     zcopies = [
-        remote(rel.at[pl.ds(0, 15)], below, zsend.at[0], zrecv.at[0], *beside(1, 0)),
-        remote(rel.at[pl.ds(5, 15)], above, zsend.at[1], zrecv.at[1], *beside(-1, 0)),
+        remote(rel.at[pl.ds(0, 10)], below, zsend.at[0], zrecv.at[0], *beside(1, 0)),
+        remote(rel.at[pl.ds(10, 10)], above, zsend.at[1], zrecv.at[1], *beside(-1, 0)),
     ]
     if_within(1, zcopies[0].start)
     if_within(-1, zcopies[1].start)
@@ -356,35 +363,32 @@
     if_within(-1, zcopies[0].wait_recv)
     if_within(1, zcopies[1].wait_recv)
     has_below, has_above = gz > 0, gz < 127
-    for q in range(20):
-        cz, i = VELOCITIES[q][0], ZPLACE[q]
-        mine = rel[i].astype(f32)
-        if cz >= 0:
-            under = jnp.where(has_below, below[i].astype(f32), 0.0)
-        if cz <= 0:
-            over = jnp.where(has_above, above[i - 5].astype(f32), 0.0)
-        if cz == 1:
-            rows = [under, mine]
-        elif cz == -1:
-            rows = [mine, over]
-        else:
-            rows = [under[8:16], mine, over[0:8]]
-        put(work, q, pl.ds(0, 32), jnp.concatenate(rows, axis=0))
+    for k in range(5):
+        under, mine = jnp.where(has_below, below[k].astype(f32), 0.0), rel[k].astype(f32)
+        put(work, UP[k], pl.ds(0, 32), jnp.concatenate([under, mine], axis=0))
+        mine, over = rel[15 + k].astype(f32), jnp.where(has_above, above[5 + k].astype(f32), 0.0)
+        put(work, DOWN[k], pl.ds(0, 32), jnp.concatenate([mine, over], axis=0))
+        under, over = jnp.where(has_below, below[5 + k].astype(f32), 0.0), jnp.where(has_above, above[k].astype(f32), 0.0)
+        upper, lower = rel[5 + k].astype(f32), rel[10 + k].astype(f32)
+        for half in (0, 1):
+            planes = [x[8 * half : 8 * half + 8] for x in (under, lower, upper, over)]
+            put(work, FLAT[2 * k + half], pl.ds(0, 32), jnp.concatenate(planes, axis=0))
 
     def column(q, x):
         return wide(work, q, pl.ds(x, 4, stride=8))
 
-    def edge_tile(q):
-        cx = VELOCITIES[q][1]
-        first_x, then_x = {0: (7, 0), 1: (7, 6), -1: (0, 1)}[cx]
-        return jnp.concatenate([column(q, first_x), column(q, then_x)], axis=0)
-
-    for b in range(11):
-        edge[b] = jnp.concatenate([edge_tile(XTILES[2 * b]), edge_tile(XTILES[2 * b + 1])], axis=0).astype(bf16)
+    def tile_of(first_tile, then_tile):
+        return jnp.concatenate([column(*first_tile), column(*then_tile)], axis=0)
+
+    flats = [(XFLAT[2 * k], XFLAT[2 * k + 1]) for k in range(5)]
+    tiles = [((q, 7), (q, 6)) for q in XUP] + [((a, 7), (b, 7)) for a, b in flats]
+    tiles += [((a, 0), (b, 0)) for a, b in flats] + [((q, 0), (q, 1)) for q in XDOWN]
+    for b in range(10):
+        edge[b] = jnp.concatenate([tile_of(*tiles[2 * b]), tile_of(*tiles[2 * b + 1])], axis=0).astype(bf16)
     to_right, to_left = beside(0, 1), beside(0, -1)
     xcopies = [
-        remote(edge.at[pl.ds(0, 8)], left, xsend.at[0], xrecv.at[0], *to_right),
-        remote(edge.at[pl.ds(3, 8)], right, xsend.at[1], xrecv.at[1], *to_left),
+        remote(edge.at[pl.ds(0, 5)], left, xsend.at[0], xrecv.at[0], *to_right),
+        remote(edge.at[pl.ds(5, 5)], right, xsend.at[1], xrecv.at[1], *to_left),
     ]
     for c in xcopies:
         c.start()
@@ -415,23 +419,22 @@
     has_left, has_right = col > 0, col < 3
     row8 = iota((8, 512), 0)
 
-    def tile(ref, shift, q, there):
-        k = XPLACE[q] - shift
-        both = jnp.where(there, ref[k // 2].astype(f32), 0.0)
-        return both[8 * (k % 2) : 8 * (k % 2) + 8]
-
-    for q in range(20):
-        cx = VELOCITIES[q][1]
-        if cx == 0:
-            put(work, q, pl.ds(32, 8), jnp.where(row8 < 4, tile(left, 0, q, has_left), tile(right, 6, q, has_right)))
-        else:
-            ends = tile(left, 0, q, has_left) if cx == 1 else tile(right, 6, q, has_right)
-            k = XPLACE[q]
-            mine = edge[k // 2].astype(f32)[8 * (k % 2) : 8 * (k % 2) + 8]
-            merged = jnp.where(row8 < 4, mine, ends)
-            put(work, q, pl.ds(32, 8), row_roll(merged, 4) if cx == 1 else merged)
-            put(work, q, pl.ds(0, 32), row_roll(wide(work, q, pl.ds(0, 32)), cx))
-            put(work, q, pl.ds(0 if cx == 1 else 7, 4, stride=8), ends[0:4])
+    def tile(ref, k, there=None):
+        both = ref[k // 2].astype(f32)[8 * (k % 2) : 8 * (k % 2) + 8]
+        return both if there is None else jnp.where(there, both, 0.0)
+
+    for k in range(5):
+        from_left, from_right = tile(left, 5 + k, has_left), tile(right, k, has_right)
+        put(work, flats[k][0], pl.ds(32, 8), jnp.where(row8 < 4, from_left, row_roll(from_right, 4)))
+        put(work, flats[k][1], pl.ds(32, 8), jnp.where(row8 < 4, row_roll(from_left, 4), from_right))
+        q, ends = XUP[k], tile(left, k, has_left)
+        put(work, q, pl.ds(32, 8), row_roll(jnp.where(row8 < 4, tile(edge, k), ends), 4))
+        put(work, q, pl.ds(0, 32), row_roll(wide(work, q, pl.ds(0, 32)), 1))
+        put(work, q, pl.ds(0, 4, stride=8), ends[0:4])
+        q, ends = XDOWN[k], tile(right, 5 + k, has_right)
+        put(work, q, pl.ds(32, 8), jnp.where(row8 < 4, tile(edge, 15 + k), ends))
+        put(work, q, pl.ds(0, 32), row_roll(wide(work, q, pl.ds(0, 32)), -1))
+        put(work, q, pl.ds(7, 4, stride=8), ends[0:4])
 
     for i, (dz, dx) in enumerate(NEAR):
         if_within(dz, ncopies[7 - i].wait_recv)
@@ -551,9 +554,8 @@
         + [pltpu.VMEM((16, 512), jnp.int32), pltpu.VMEM((19, 16, 512), bf16)]
         + [pltpu.VMEM((128, 128), f32), pltpu.VMEM((2, 128, 128), f32)] * 2
         + [pltpu.VMEM((20, 16, 512), bf16)]
-        + [pltpu.VMEM((15, 16, 512), bf16)] * 2
-        + [pltpu.VMEM((11, 16, 512), bf16)]
-        + [pltpu.VMEM((8, 16, 512), bf16)] * 2
+        + [pltpu.VMEM((10, 16, 512), bf16)] * 3
+        + [pltpu.VMEM((5, 16, 512), bf16)] * 2
         + [pltpu.VMEM((16, 512), bf16), pltpu.VMEM((8, 16, 512), bf16)]
         + [pltpu.VMEM((3, 4, 96, 128), f32)]
         + [pltpu.VMEM((20, 4, 40, 128), f32)] * 2

time: 31.8 us -> 30.8 us (0.969)
  Pallas kernels: 31.1 us -> 30 us
    pallas_call x1, Pallas kernels: 30.3 us -> 29.3 us  [body(): pl.pallas_call(step_pair, out_shape=(jax.ShapeDtypeStruct((19, 16, 512),...]
where the time goes in v6:
time: 30.8 us; the launch traced here: 30.7 us
  Pallas kernels  30 us (97%)
  between operations  0.64 us (2%)
    pallas_call x1, Pallas kernels, body(): pl.pallas_call(step_pair, out_shape=(jax.ShapeDtypeStruct((19, 16, 512),...  29.3 us
    pallas_call x1, Pallas kernels, body(): pl.pallas_call(hand_over, out_shape=(jax.ShapeDtypeStruct((19, 16, 512),...  0.75 us

profile of v6, /device:TPU:1, one launch (start us, length us, event | category | flops | bytes accessed | tf_op | source)
XLA Modules:
  0.0 30.7 jit_solution(14724215326551988672)
XLA Ops:
  0.6 29.3 %two_steps.1 = (bf16[19,16,512]{2,1,0:T(8,128)(2,1)S(1)}, f32[2,128]{1,0:T(2,128)S(1)}, f32[2,128]{1,0:T(2,128)S(1)}) custom-call(s32[2,128]{1,0:T(2,128)} %bitcast.12, s32[2,128]{1,0:T(2,128)} %bitcast.13, f32[2,128]{1,0:T(2,128)} %bitcast.14, f32[2,128]{1,0:T(2,128)} %bitcast.15, f32[2,128]{1,0:T(2,128)} %bitcast.16, s32[16,512]{1,0:T(8,128)} %bitcast.11, ...), custom_call_target="tpu_custom_call" | custom-call | tf_op jit(solution)/shard_map/two_steps/pallas_call | solution.py:548
  29.9 0.8 %hand_over.1 = (bf16[19,16,512]{2,1,0:T(8,128)(2,1)}, f32[2,128]{1,0:T(2,128)}, f32[2,128]{1,0:T(2,128)}) custom-call(bf16[19,16,512]{2,1,0:T(8,128)(2,1)S(1)} %get-tuple-element.9.a, f32[2,128]{1,0:T(2,128)S(1)} %get-tuple-element.10.b, f32[2,128]{1,0:T(2,128)S(1)} %get-tuple-element.11.c), custom_call_target="tpu_custom_call" | custom-call | tf_op jit(solution)/shard_map/hand_over/pallas_call | solution.py:570
